TPU v7x, 128 devices: a whole 4x4x4 slice. The times are simulated.
128 devices in a mesh: row: 16 (over x, z), col: 8 (over y, core).
Axes of the slice: x: 4, y: 4, z: 4, core: 2. Of those that a mesh axis runs over, the one named last changes fastest.
Arguments:
- fine_input: bfloat16 [1024, 1024, 128], P('row', 'col'), may hold values from -6 to 6
- interp_weights: bfloat16 [1024, 1024, 128], P('row', 'col'), may hold values from -0.5 to 0.5
- intersection_ids: int32 [16, 8, 16], P('row', 'col'), may hold values from 0 to 4095, as said below
- live_counts: int32 [16, 8], P('row', 'col'), may hold values from 10 to 16
- coarse_state: bfloat16 [32768, 100], P('row'), may hold values from -6 to 6
- cond_weight: bfloat16 [100, 128], replicated, may hold values from -0.625 to 0.625
- conv_one: bfloat16 [3, 3, 128, 128], replicated, may hold values from -0.1875 to 0.1875
- conv_two: bfloat16 [3, 3, 128, 128], replicated, may hold values from -0.1875 to 0.1875
- cot_one: bfloat16 [1024, 1024, 128], P('row', 'col'), may hold values from -6 to 6
- cot_two: bfloat16 [512, 512, 128], P('row', 'col'), may hold values from -6 to 6
Outputs:
- skip_two: bfloat16 [512, 512, 128], P('row', 'col')
- grad_input: bfloat16 [1024, 1024, 128], P('row', 'col')
- grad_conv_one: float32 [3, 3, 128, 128], replicated
- grad_conv_two: float32 [3, 3, 128, 128], replicated
- grad_cond: float32 [100, 128], replicated
- grad_coarse: float32 [32768, 100], P('row')
Inputs may be any that keep to these rules, and one draw needn't show every extreme that they name: `intersection_ids`: block ids; block b lies on coarse shard b // 256. At most 2 of the 16 entries of one tile name blocks of one shard, and some shard is named 2 times by every tile; a block may be listed more than once.
All inputs are finite; a program needn't handle non-finite values.
Results may differ from a plain program's by a relative error of at most 0.015.
Values may be sent and summed in bfloat16 or wider, within the bound.
A program may use at most 128 MiB of HBM per device.

v0:
```python
import jax
import jax.numpy as jnp
from jax import lax
from jax.sharding import PartitionSpec as P

CB = 8
CAP = 2


def extended(block, sides, width):
    for axis, dim in sides:
        count = lax.axis_size(axis)
        forward = [(i, i + 1) for i in range(count - 1)]
        backward = [(target, source) for source, target in forward]
        low = lax.ppermute(
            lax.slice_in_dim(block, block.shape[dim] - width, None, axis=dim), axis, forward
        )
        high = lax.ppermute(lax.slice_in_dim(block, 0, width, axis=dim), axis, backward)
        block = jnp.concatenate([low, block, high], axis=dim)
    return block


def silu_slope(field):
    sig = jax.nn.sigmoid(field)
    return sig * (1.0 + field * (1.0 - sig))


def forward_conv(field, weight):
    height, breadth, channels = field.shape
    padded = extended(field, (("row", 0), ("col", 1)), 1)
    running = jnp.zeros((height * breadth, weight.shape[3]), jnp.float32)
    for row_tap in range(3):
        for col_tap in range(3):
            window = padded[row_tap : row_tap + height, col_tap : col_tap + breadth].reshape(
                -1, channels
            )
            running = running + jnp.dot(
                window, weight[row_tap, col_tap], preferred_element_type=jnp.float32
            )
    return (running.reshape(height, breadth, -1), padded)


def backward_conv(delta, weight):
    height, breadth, channels = delta.shape
    padded = extended(delta, (("row", 0), ("col", 1)), 1)
    running = jnp.zeros((height * breadth, weight.shape[2]), jnp.float32)
    for row_tap in range(3):
        for col_tap in range(3):
            window = padded[
                2 - row_tap : 2 - row_tap + height, 2 - col_tap : 2 - col_tap + breadth
            ].reshape(-1, channels)
            running = running + jnp.dot(
                window, weight[row_tap, col_tap].T, preferred_element_type=jnp.float32
            )
    return running.reshape(height, breadth, -1)


def tap_grad(padded, delta):
    height, breadth, channels = delta.shape
    flat_delta = delta.reshape(-1, channels)
    tap_rows = []
    for row_tap in range(3):
        tap_line = []
        for col_tap in range(3):
            window = padded[row_tap : row_tap + height, col_tap : col_tap + breadth].reshape(
                -1, padded.shape[2]
            )
            tap_line.append(
                jnp.einsum("nc,nd->cd", window, flat_delta, preferred_element_type=jnp.float32)
            )
        tap_rows.append(jnp.stack(tap_line))
    return jnp.stack(tap_rows)


def pool_pairs(field):
    height, breadth, channels = field.shape
    grouped = field.astype(jnp.float32).reshape(height // 2, 2, breadth // 2, 2, channels)
    return (jnp.sum(grouped, axis=(1, 3)) * 0.25).astype(jnp.bfloat16)


def spread_pairs(field):
    return jnp.repeat(jnp.repeat(field, 2, axis=0), 2, axis=1) * 0.25


def per_device(
    fine_input,
    interp_weights,
    intersection_ids,
    live_counts,
    coarse_state,
    cond_weight,
    conv_one,
    conv_two,
    cot_one,
    cot_two,
):
    highest = lax.Precision.HIGHEST
    row_count = lax.axis_size("row")
    tile_height, tile_width, channels = fine_input.shape
    coarse_channels = coarse_state.shape[1]
    blocks_dev = coarse_state.shape[0] // CB
    listed_ids = intersection_ids.reshape(-1)
    listed = listed_ids.shape[0]
    live_total = live_counts.reshape(())
    slot_number = jnp.arange(listed)
    live_slot = slot_number < live_total
    owner_shard = listed_ids // blocks_dev
    local_block = listed_ids % blocks_dev
    earlier = (owner_shard[:, None] == owner_shard[None, :]) & (
        slot_number[None, :] < slot_number[:, None]
    )
    slot_rank = jnp.sum(earlier.astype(jnp.int32), axis=1)
    slot_place = jnp.where(live_slot, owner_shard * CAP + slot_rank, -1)
    hit_mask = slot_place[:, None] == jnp.arange(row_count * CAP)[None, :]
    request = jnp.sum(jnp.where(hit_mask, local_block[:, None] + 1, 0), axis=0) - 1
    asked_ids = lax.all_to_all(
        request.reshape(row_count, CAP), "row", split_axis=0, concat_axis=0, tiled=True
    ).reshape(-1)
    asked_valid = asked_ids >= 0
    stored = coarse_state.reshape(blocks_dev, CB, coarse_channels)
    picked = jnp.take(stored, jnp.clip(asked_ids, 0, blocks_dev - 1), axis=0)
    picked = jnp.where(asked_valid[:, None, None], picked, jnp.zeros_like(picked))
    hit_table = hit_mask.astype(jnp.float32)
    row_live = jnp.repeat(live_slot, CB)
    safe_place = jnp.clip(slot_place, 0, row_count * CAP - 1)
    arrived = lax.all_to_all(
        picked.reshape(row_count, CAP, CB, coarse_channels),
        "row",
        split_axis=0,
        concat_axis=0,
        tiled=True,
    )
    patches = jnp.take(
        arrived.reshape(row_count * CAP, CB, coarse_channels), safe_place, axis=0
    ).reshape(-1, coarse_channels)
    patches = jnp.where(row_live[:, None], patches, jnp.zeros_like(patches))
    projected = jnp.dot(patches, cond_weight, preferred_element_type=jnp.float32).astype(
        jnp.bfloat16
    )
    interp_flat = interp_weights.reshape(-1, interp_weights.shape[2])
    condition = jnp.dot(interp_flat, projected, preferred_element_type=jnp.float32).reshape(
        tile_height, tile_width, channels
    )
    level_one_in = (fine_input.astype(jnp.float32) + condition).astype(jnp.bfloat16)
    z_one, pad_one = forward_conv(level_one_in, conv_one)
    y_one = jax.nn.silu(z_one).astype(jnp.bfloat16)
    level_two_in = pool_pairs(y_one)
    z_two, pad_two = forward_conv(level_two_in, conv_two)
    skip_two = jax.nn.silu(z_two).astype(jnp.bfloat16)
    delta_two = (cot_two.astype(jnp.float32) * silu_slope(z_two)).astype(jnp.bfloat16)
    grad_two = tap_grad(pad_two, delta_two)
    back_two = backward_conv(delta_two, conv_two)
    delta_one = ((cot_one.astype(jnp.float32) + spread_pairs(back_two)) * silu_slope(z_one)).astype(
        jnp.bfloat16
    )
    grad_one = tap_grad(pad_one, delta_one)
    grad_input = backward_conv(delta_one, conv_one).astype(jnp.bfloat16)
    grad_projected = jnp.einsum(
        "nj,nc->jc",
        interp_flat,
        grad_input.reshape(-1, channels),
        preferred_element_type=jnp.float32,
    ).astype(jnp.bfloat16)
    grad_projected = jnp.where(row_live[:, None], grad_projected, jnp.zeros_like(grad_projected))
    grad_cond = jnp.einsum("nd,nc->dc", patches, grad_projected, preferred_element_type=jnp.float32)
    grad_patch = jnp.dot(grad_projected, cond_weight.T, preferred_element_type=jnp.float32).reshape(
        listed, CB, coarse_channels
    )
    placed = jnp.einsum("kp,kbd->pbd", hit_table, grad_patch, precision=highest)
    grad_picked = (
        lax.all_to_all(
            placed.reshape(row_count, CAP, CB, coarse_channels).astype(jnp.bfloat16),
            "row",
            split_axis=0,
            concat_axis=0,
            tiled=True,
        )
        .astype(jnp.float32)
        .reshape(row_count * CAP, CB, coarse_channels)
    )
    owner_table = (asked_ids[:, None] == jnp.arange(blocks_dev)[None, :]).astype(jnp.float32)
    coarse_part = jnp.einsum("pk,pbd->kbd", owner_table, grad_picked, precision=highest).reshape(
        -1, coarse_channels
    )
    grad_coarse = lax.psum(coarse_part.astype(jnp.bfloat16), "col").astype(jnp.float32)
    total_one, total_two, total_cond = lax.psum((grad_one, grad_two, grad_cond), ("row", "col"))
    return (skip_two, grad_input, total_one, total_two, total_cond, grad_coarse)


def solution(mesh):
    placed = (
        P("row", "col", None),
        P("row", "col", None),
        P("row", "col", None),
        P("row", "col"),
        P("row", None),
        P(),
        P(),
        P(),
        P("row", "col", None),
        P("row", "col", None),
    )
    return jax.shard_map(
        per_device,
        mesh=mesh,
        in_specs=placed,
        out_specs=(P("row", "col", None), P("row", "col", None), P(), P(), P(), P("row", None)),
        check_vma=False,
    )
```

profile of v0, /device:TPU:1, one launch (start us, length us, event | category | flops | bytes accessed | tf_op | source)
XLA Modules:
  0.0 492.6 jit_solution(17706056963797202746)
XLA Ops:
  10.2 8.4 %all-to-all-start = ((s32[16,1,2]{2,1,0:T(1,128)}), s32[16,1,2]{2,1,0:T(1,128)S(1)}, u32[]{:S(2)}, u32[]{:S(2)}) async-start(s32[16,1,2]{2,1,0:T(1,128)} %bitcast.2), calls=%async_computation | async-start | bytes 16384 | tf_op jit(solution)/shard_map/all_to_all | solution.py:116
  20.6 4.4 all-to-all-done
  26.8 3.5 all-to-all-start.1
  30.7 4.1 copy.132
  40.3 3.5 fusion.2
  48.6 4.1 copy.149
  60.0 7.1 %collective-permute-start.2 = (bf16[66,1,128]{2,0,1:T(8,128)(2,1)S(1)}, bf16[66,1,128]{2,0,1:T(8,128)(2,1)S(1)}, u32[]{:S(2)}, u32[]{:S(2)}) collective-permute-start(bf16[66,1,128]{2,0,1:T(8,128)(2,1)S(1)} %copy.141), channel_id=1, source_target_pairs={{0,1},{1,2},{2,3},{3,4},{4,5},{5,6},{6,7},{8,9},{9,10},{10,11},{11... | collective-permute-start | bytes 50696 | tf_op jit(solution)/shard_map/ppermute | solution.py:15
  71.6 4.7 pad_maximum_fusion.5
  76.2 4.1 copy.144
  80.3 4.1 copy.152
  88.4 8.8 %pad_maximum_fusion = (bf16[66,129,128]{1,2,0:T(8,128)(2,1)}, bf16[66,129,128]{1,2,0:T(8,128)(2,1)S(1)}) fusion(bf16[66,1,128]{1,2,0:T(8,128)(2,1)} %copy.146, bf16[1,128,128]{1,2,0:T(8,128)(2,1)S(1)} %collective-permute-done.1, bf16[64,128,128]{1,2,0:T(8,128)(2,1)} %copy-done.1, bf16[1,128,128]{1,2,0:T(8,128)(2,1)S(1)} %collective-permute-done, ...), kind=kLoop, calls=%fused_computation.20 | loop fusion | flops 17436672 | bytes 6555648 | tf_op jit(solution)/shard_map/concatenate | solution.py:19
  97.2 4.2 fusion.144
  101.4 4.1 copy.143
  105.5 7.9 %fusion.143 = (bf16[64,128,128]{1,2,0:T(8,128)(2,1)}, bf16[64,128,128]{1,2,0:T(8,128)(2,1)}, bf16[64,128,128]{1,2,0:T(8,128)(2,1)}) fusion(bf16[66,129,128]{1,2,0:T(8,128)(2,1)} %get-tuple-element.56), kind=kLoop, calls=%fused_computation.264 | loop fusion | bytes 12582912 | tf_op jit(solution)/shard_map/slice | solution.py:34
  113.3 4.1 copy.147
  117.4 4.1 copy.148
  121.5 4.1 copy.150
  125.6 4.1 copy.151
  129.7 4.6 copy.153
  150.8 3.8 collective-permute-start.4
  159.2 5.1 %collective-permute-start.6 = (bf16[34,1,128]{2,1,0:T(2,128)(2,1)S(1)}, bf16[34,1,128]{2,1,0:T(2,128)(2,1)S(1)}, u32[]{:S(2)}, u32[]{:S(2)}) collective-permute-start(bf16[34,1,128]{2,1,0:T(2,128)(2,1)S(1)} %get-tuple-element.88), channel_id=1, source_target_pairs={{0,1},{1,2},{2,3},{3,4},{4,5},{5,6},{6,7},{8,9},{9,10},{10,11},{11... | collective-permute-start | bytes 26120 | tf_op jit(solution)/shard_map/ppermute | solution.py:15
  177.2 3.6 collective-permute-start.8
  187.7 3.9 collective-permute-start.11
  196.0 3.5 broadcast_in_dim.106
  199.5 3.7 multiply_convert_fusion
  203.2 3.3 convolution_bitcast_fusion.17
  218.2 5.7 %collective-permute-start.12 = (bf16[1,128,128]{2,1,0:T(8,128)(2,1)S(1)}, bf16[1,128,128]{2,1,0:T(8,128)(2,1)S(1)}, u32[]{:S(2)}, u32[]{:S(2)}) collective-permute-start(bf16[1,128,128]{2,1,0:T(8,128)(2,1)S(1)} %get-tuple-element.62), channel_id=1, source_target_pairs={{0,8},{8,16},{16,24},{24,32},{32,40},{40,48},{48,56},{56,64},{64,7... | collective-permute-start | bytes 98312 | tf_op jit(solution)/shard_map/ppermute | solution.py:15
  230.8 5.5 %collective-permute-start.15 = (bf16[66,1,128]{2,1,0:T(2,128)(2,1)S(1)}, bf16[66,1,128]{2,1,0:T(2,128)(2,1)S(1)}, u32[]{:S(2)}, u32[]{:S(2)}) collective-permute-start(bf16[66,1,128]{2,1,0:T(2,128)(2,1)S(1)} %get-tuple-element.55), channel_id=1, source_target_pairs={{0,1},{1,2},{2,3},{3,4},{4,5},{5,6},{6,7},{8,9},{9,10},{10,11},{11... | collective-permute-start | bytes 50696 | tf_op jit(solution)/shard_map/ppermute | solution.py:15
  251.3 8.2 %all-to-all-start.2 = ((bf16[16,2,8,100]{3,2,1,0:T(8,128)(2,1)}), bf16[16,2,8,100]{3,2,1,0:T(8,128)(2,1)S(1)}, u32[]{:S(2)}, u32[]{:S(2)}) async-start(bf16[16,2,8,100]{3,2,1,0:T(8,128)(2,1)} %copy.159), calls=%async_computation.2 | async-start | bytes 131072 | tf_op jit(solution)/shard_map/all_to_all | solution.py:171
  259.5 6.4 %all-to-all-done.2 = bf16[16,2,8,100]{3,2,1,0:T(8,128)(2,1)S(1)} async-done(((bf16[16,2,8,100]{3,2,1,0:T(8,128)(2,1)}), bf16[16,2,8,100]{3,2,1,0:T(8,128)(2,1)S(1)}, u32[]{:S(2)}, u32[]{:S(2)}) %all-to-all-start.2) | async-done | bytes 51232 | tf_op jit(solution)/shard_map/all_to_all | solution.py:171
  268.7 65.6 %psum.30 = f32[100,128]{1,0:T(8,128)} all-reduce(f32[100,128]{1,0:T(8,128)S(1)} %fusion.127), channel_id=1, replica_groups=mesh['row'=16,'col'=8] {'row','col'}, use_global_device_ids=true, to_apply=%region_5.6 | all-reduce | flops 12800 | bytes 102400 | tf_op jit(solution)/shard_map/psum | solution.py:186
  336.5 145.0 %all-reduce.6.cloned.1.call-done = (f32[3,3,128,128]{3,2,1,0:T(8,128)}, f32[3,3,128,128]{3,2,1,0:T(8,128)}) async-done(((f32[3,3,128,128]{3,2,1,0:T(8,128)}, f32[3,3,128,128]{3,2,1,0:T(8,128)}), (f32[3,3,128,128]{3,2,1,0:T(8,128)}, f32[3,3,128,128]{3,2,1,0:T(8,128)})) %all-reduce.6.cloned.1.call-update) | async-done | bytes 1179664 | tf_op jit(solution)/shard_map/psum | solution.py:186
  (223 shorter events, 119.4 us)
Async XLA Ops:
  7.2 30.2 %copy-start = (bf16[64,128,128]{2,1,0:T(8,128)(2,1)S(1)}, bf16[64,128,128]{2,1,0:T(8,128)(2,1)}, u32[]{:S(2)}) copy-start(bf16[64,128,128]{2,1,0:T(8,128)(2,1)} %param.11) | copy-start | bytes 6291460
  10.2 14.8 %all-to-all-start = ((s32[16,1,2]{2,1,0:T(1,128)}), s32[16,1,2]{2,1,0:T(1,128)S(1)}, u32[]{:S(2)}, u32[]{:S(2)}) async-start(s32[16,1,2]{2,1,0:T(1,128)} %bitcast.2), calls=%async_computation | async-start | bytes 16384 | tf_op jit(solution)/shard_map/all_to_all | solution.py:116
  26.8 10.0 %all-to-all-start.1 = ((bf16[16,2,8,100]{3,2,1,0:T(8,128)(2,1)}), bf16[16,2,8,100]{3,2,1,0:T(8,128)(2,1)S(1)}, u32[]{:S(2)}, u32[]{:S(2)}) async-start(bf16[16,2,8,100]{3,2,1,0:T(8,128)(2,1)} %select_select_fusion), calls=%async_computation.1 | async-start | bytes 131072 | tf_op jit(solution)/shard_map/all_to_all | solution.py:126
  30.5 6.9 %copy-start.22 = (pred[128]{0:T(512)(128)(4,1)}, pred[128]{0:T(512)(128)(4,1)S(1)}, u32[]{:S(2)}) copy-start(pred[128]{0:T(512)(128)(4,1)S(1)} %broadcast_in_dim.92) | copy-start | bytes 388
  30.7 6.7 %copy-start.24 = (pred[128]{0:T(512)(128)(4,1)}, pred[128]{0:T(512)(128)(4,1)S(1)}, u32[]{:S(2)}) copy-start(pred[128]{0:T(512)(128)(4,1)S(1)} %broadcast_in_dim.95) | copy-start | bytes 388
  30.7 6.7 %copy-start.20 = (bf16[100,128]{1,0:T(8,128)(2,1)S(1)}, bf16[100,128]{1,0:T(8,128)(2,1)}, u32[]{:S(2)}) copy-start(bf16[100,128]{1,0:T(8,128)(2,1)} %param.15) | copy-start | bytes 76804
  37.3 3.0 copy-start.18
  45.1 7.6 %collective-permute-start = (bf16[1,128,128]{1,2,0:T(8,128)(2,1)S(1)}, bf16[1,128,128]{1,2,0:T(8,128)(2,1)S(1)}, u32[]{:S(2)}, u32[]{:S(2)}) collective-permute-start(bf16[1,128,128]{1,2,0:T(8,128)(2,1)S(1)} %get-tuple-element.66), channel_id=1, source_target_pairs={{0,8},{8,16},{16,24},{24,32},{32,40},{40,48},{48,56},{56,64},{64,7... | collective-permute-start | bytes 98312 | tf_op jit(solution)/shard_map/ppermute | solution.py:15
  47.3 5.4 %collective-permute-start.1 = (bf16[1,128,128]{1,2,0:T(8,128)(2,1)S(1)}, bf16[1,128,128]{1,2,0:T(8,128)(2,1)S(1)}, u32[]{:S(2)}, u32[]{:S(2)}) collective-permute-start(bf16[1,128,128]{1,2,0:T(8,128)(2,1)S(1)} %get-tuple-element.67), channel_id=1, source_target_pairs={{8,0},{16,8},{24,16},{32,24},{40,32},{48,40},{56,48},{64,56},{72,6... | collective-permute-start | bytes 98312 | tf_op jit(solution)/shard_map/ppermute | solution.py:18
  60.0 24.4 %collective-permute-start.2 = (bf16[66,1,128]{2,0,1:T(8,128)(2,1)S(1)}, bf16[66,1,128]{2,0,1:T(8,128)(2,1)S(1)}, u32[]{:S(2)}, u32[]{:S(2)}) collective-permute-start(bf16[66,1,128]{2,0,1:T(8,128)(2,1)S(1)} %copy.141), channel_id=1, source_target_pairs={{0,1},{1,2},{2,3},{3,4},{4,5},{5,6},{6,7},{8,9},{9,10},{10,11},{11... | collective-permute-start | bytes 50696 | tf_op jit(solution)/shard_map/ppermute | solution.py:15
  69.3 17.1 %collective-permute-start.3 = (bf16[66,1,128]{2,0,1:T(8,128)(2,1)S(1)}, bf16[66,1,128]{2,0,1:T(8,128)(2,1)S(1)}, u32[]{:S(2)}, u32[]{:S(2)}) collective-permute-start(bf16[66,1,128]{2,0,1:T(8,128)(2,1)S(1)} %copy.145), channel_id=1, source_target_pairs={{1,0},{2,1},{3,2},{4,3},{5,4},{6,5},{7,6},{9,8},{10,9},{11,10},{12... | collective-permute-start | bytes 50696 | tf_op jit(solution)/shard_map/ppermute | solution.py:18
  97.2 4.2 copy-start.5
  129.7 4.6 copy-start.15
  150.7 15.8 %copy-start.16 = (bf16[3,3,128,128]{3,2,1,0:T(8,128)(2,1)S(1)}, bf16[3,3,128,128]{3,2,1,0:T(8,128)(2,1)}, u32[]{:S(2)}) copy-start(bf16[3,3,128,128]{3,2,1,0:T(8,128)(2,1)} %param.17) | copy-start | bytes 884740
  150.8 6.4 %collective-permute-start.4 = (bf16[1,64,128]{2,1,0:T(8,128)(2,1)S(1)}, bf16[1,64,128]{2,1,0:T(8,128)(2,1)S(1)}, u32[]{:S(2)}, u32[]{:S(2)}) collective-permute-start(bf16[1,64,128]{2,1,0:T(8,128)(2,1)S(1)} %get-tuple-element.96), channel_id=1, source_target_pairs={{0,8},{8,16},{16,24},{24,32},{32,40},{40,48},{48,56},{56,64},{64,7... | collective-permute-start | bytes 49160 | tf_op jit(solution)/shard_map/ppermute | solution.py:15
  154.7 4.5 collective-permute-start.5
  159.2 7.5 %collective-permute-start.6 = (bf16[34,1,128]{2,1,0:T(2,128)(2,1)S(1)}, bf16[34,1,128]{2,1,0:T(2,128)(2,1)S(1)}, u32[]{:S(2)}, u32[]{:S(2)}) collective-permute-start(bf16[34,1,128]{2,1,0:T(2,128)(2,1)S(1)} %get-tuple-element.88), channel_id=1, source_target_pairs={{0,1},{1,2},{2,3},{3,4},{4,5},{5,6},{6,7},{8,9},{9,10},{10,11},{11... | collective-permute-start | bytes 26120 | tf_op jit(solution)/shard_map/ppermute | solution.py:15
  164.3 5.1 %collective-permute-start.7 = (bf16[34,1,128]{2,1,0:T(2,128)(2,1)S(1)}, bf16[34,1,128]{2,1,0:T(2,128)(2,1)S(1)}, u32[]{:S(2)}, u32[]{:S(2)}) collective-permute-start(bf16[34,1,128]{2,1,0:T(2,128)(2,1)S(1)} %get-tuple-element.89), channel_id=1, source_target_pairs={{1,0},{2,1},{3,2},{4,3},{5,4},{6,5},{7,6},{9,8},{10,9},{11,10},{12... | collective-permute-start | bytes 26120 | tf_op jit(solution)/shard_map/ppermute | solution.py:18
  177.2 6.5 %collective-permute-start.8 = (bf16[1,64,128]{2,1,0:T(8,128)(2,1)S(1)}, bf16[1,64,128]{2,1,0:T(8,128)(2,1)S(1)}, u32[]{:S(2)}, u32[]{:S(2)}) collective-permute-start(bf16[1,64,128]{2,1,0:T(8,128)(2,1)S(1)} %get-tuple-element.92), channel_id=1, source_target_pairs={{0,8},{8,16},{16,24},{24,32},{32,40},{40,48},{48,56},{56,64},{64,7... | collective-permute-start | bytes 49160 | tf_op jit(solution)/shard_map/ppermute | solution.py:15
  180.8 5.0 %collective-permute-start.9 = (bf16[1,64,128]{2,1,0:T(8,128)(2,1)S(1)}, bf16[1,64,128]{2,1,0:T(8,128)(2,1)S(1)}, u32[]{:S(2)}, u32[]{:S(2)}) collective-permute-start(bf16[1,64,128]{2,1,0:T(8,128)(2,1)S(1)} %get-tuple-element.93), channel_id=1, source_target_pairs={{8,0},{16,8},{24,16},{32,24},{40,32},{48,40},{56,48},{64,56},{72,6... | collective-permute-start | bytes 49160 | tf_op jit(solution)/shard_map/ppermute | solution.py:18
  185.8 6.2 %collective-permute-start.10 = (bf16[34,1,128]{2,1,0:T(2,128)(2,1)S(1)}, bf16[34,1,128]{2,1,0:T(2,128)(2,1)S(1)}, u32[]{:S(2)}, u32[]{:S(2)}) collective-permute-start(bf16[34,1,128]{2,1,0:T(2,128)(2,1)S(1)} %get-tuple-element.84), channel_id=1, source_target_pairs={{1,0},{2,1},{3,2},{4,3},{5,4},{6,5},{7,6},{9,8},{10,9},{11,10},{12... | collective-permute-start | bytes 26120 | tf_op jit(solution)/shard_map/ppermute | solution.py:18
  187.7 4.5 collective-permute-start.11
  196.0 3.5 copy-start.4
  203.2 8.8 %slice-start = ((s8[4325376]{0:T(1024)(128)(4,1)}), s8[4194304]{0:T(1024)(128)(4,1)S(1)}, s32[]{:S(2)}) async-start(s8[4325376]{0:T(1024)(128)(4,1)} %bitcast.352), calls=%async_computation.5 | async-start | bytes 8388608
  206.5 5.5 %slice-start.1 = ((s8[4325376]{0:T(1024)(128)(4,1)}), s8[131072]{0:T(1024)(128)(4,1)S(1)}, s32[]{:S(2)}) async-start(s8[4325376]{0:T(1024)(128)(4,1)} %bitcast.352), calls=%async_computation.6 | async-start | bytes 262144
  218.2 8.8 %collective-permute-start.12 = (bf16[1,128,128]{2,1,0:T(8,128)(2,1)S(1)}, bf16[1,128,128]{2,1,0:T(8,128)(2,1)S(1)}, u32[]{:S(2)}, u32[]{:S(2)}) collective-permute-start(bf16[1,128,128]{2,1,0:T(8,128)(2,1)S(1)} %get-tuple-element.62), channel_id=1, source_target_pairs={{0,8},{8,16},{16,24},{24,32},{32,40},{40,48},{48,56},{56,64},{64,7... | collective-permute-start | bytes 98312 | tf_op jit(solution)/shard_map/ppermute | solution.py:15
  224.0 4.7 collective-permute-start.13
  228.7 8.6 %collective-permute-start.14 = (bf16[66,1,128]{2,1,0:T(2,128)(2,1)S(1)}, bf16[66,1,128]{2,1,0:T(2,128)(2,1)S(1)}, u32[]{:S(2)}, u32[]{:S(2)}) collective-permute-start(bf16[66,1,128]{2,1,0:T(2,128)(2,1)S(1)} %get-tuple-element.54), channel_id=1, source_target_pairs={{1,0},{2,1},{3,2},{4,3},{5,4},{6,5},{7,6},{9,8},{10,9},{11,10},{12... | collective-permute-start | bytes 50696 | tf_op jit(solution)/shard_map/ppermute | solution.py:18
  230.8 6.5 %collective-permute-start.15 = (bf16[66,1,128]{2,1,0:T(2,128)(2,1)S(1)}, bf16[66,1,128]{2,1,0:T(2,128)(2,1)S(1)}, u32[]{:S(2)}, u32[]{:S(2)}) collective-permute-start(bf16[66,1,128]{2,1,0:T(2,128)(2,1)S(1)} %get-tuple-element.55), channel_id=1, source_target_pairs={{0,1},{1,2},{2,3},{3,4},{4,5},{5,6},{6,7},{8,9},{9,10},{10,11},{11... | collective-permute-start | bytes 50696 | tf_op jit(solution)/shard_map/ppermute | solution.py:15
  251.3 14.7 %all-to-all-start.2 = ((bf16[16,2,8,100]{3,2,1,0:T(8,128)(2,1)}), bf16[16,2,8,100]{3,2,1,0:T(8,128)(2,1)S(1)}, u32[]{:S(2)}, u32[]{:S(2)}) async-start(bf16[16,2,8,100]{3,2,1,0:T(8,128)(2,1)} %copy.159), calls=%async_computation.2 | async-start | bytes 131072 | tf_op jit(solution)/shard_map/all_to_all | solution.py:171
  259.5 74.8 %all-reduce.4.cloned.1.call-start = ((), (), s32[]{:S(2)}) async-start(), calls=%async_computation.3 | async-start | bytes 1048576 | tf_op jit(solution)/shard_map/psum | solution.py:185
  267.5 214.0 %all-reduce.6.cloned.1.call-start = ((), (), s32[]{:S(2)}) async-start(), calls=%async_computation.4 | async-start | bytes 2359296 | tf_op jit(solution)/shard_map/psum | solution.py:186
  (19 other events, 29.3 us)
Sparse Core Ops, SparseCore 0:
  267.6 58.5 all-reduce.3
  332.4 149.0 all-reduce.5
where the time goes:
time: 499 us; the launch traced here: 493 us
  waiting for transfers between devices  166 us (33%)
  local copies, waits for them, and re-layouts  96.2 us (19%)
  starting transfers between devices  70.7 us (14%)
  blocking collectives  65.6 us (13%)
  matrix products  43 us (9%)
  other arithmetic  34.6 us (7%)
  between operations  16.2 us (3%)
    psum x1, waiting for transfers between devices, per_device(): lax.psum((grad_one, grad_two, grad_cond), ('row', 'col'))  145 us
    psum x1, blocking collectives, per_device(): lax.psum((grad_one, grad_two, grad_cond), ('row', 'col'))  65.6 us
    slice x12, local copies, waits for them, and re-layouts, forward_conv(): padded[row_tap:row_tap + height, col_tap:col_tap + breadth]  45.9 us
    ppermute x8, starting transfers between devices, extended(): lax.ppermute(lax.slice_in_dim(block, block.shape[dim] - width, None, axis...  36.8 us
    unnamed x65, local copies, waits for them, and re-layouts  22.2 us
    dot_general x18, matrix products, tap_grad(): jnp.einsum('nc,nd->cd', window, flat_delta, preferred_element_type=jnp.fl...  18.6 us
    concatenate x7, other arithmetic, extended(): block = jnp.concatenate([low, block, high], axis=dim)  14.6 us
    ppermute x8, starting transfers between devices, extended(): lax.ppermute(lax.slice_in_dim(block, 0, width, axis=dim), axis, backward)  13.7 us
  transfers between devices with their start and end apart: 21, of which 9 were waited for; matrix products, arithmetic and copies ran while one was open for 8% of the time, Pallas kernels for 0%

commit v1 on v0

v1 whole, which is shorter than its diff:
```python
import functools

import jax
import jax.numpy as jnp
from jax import lax
from jax.experimental import pallas as pl
from jax.experimental.pallas import tpu as pltpu
from jax.sharding import PartitionSpec as P

MESH = pl.DeviceIdType.MESH
BF = jnp.bfloat16
F32 = jnp.float32
CB = 8
CAP = 2
SLOT = CAP * CB
CONTRACT0 = (((0,), (0,)), ((), ()))
CONTRACT1 = (((1,), (1,)), ((), ()))


def dot(left, right):
    return jnp.dot(left, right, preferred_element_type=F32)


def iota(shape, dim):
    return lax.broadcasted_iota(jnp.int32, shape, dim)


class Push:
    def __init__(self, coords, axis, count, source, target, send, recv):
        self.coords, self.axis, self.count = coords, axis, count
        self.source, self.target, self.send, self.recv = source, target, send, recv
        self.me = coords[axis]

    def device(self, index):
        return (index, self.coords[1]) if self.axis == 0 else (self.coords[0], index)

    def copy(self, step, slot):
        peer = lax.rem(self.me + step, self.count)
        return pltpu.make_async_remote_copy(
            src_ref=self.source(peer),
            dst_ref=self.target.at[slot],
            send_sem=self.send.at[step],
            recv_sem=self.recv.at[step],
            device_id=self.device(peer),
            device_id_type=MESH,
        )

    def each(self, act):
        def body(step, carry):
            act(step)
            return carry

        lax.fori_loop(1, self.count, body, 0)

    def start(self):
        self.each(lambda step: self.copy(step, self.me).start())

    def wait_recv(self):
        self.each(
            lambda step: self.copy(step, lax.rem(self.me + self.count - step, self.count)).wait_recv()
        )

    def wait_send(self):
        self.each(lambda step: self.copy(step, self.me).wait_send())


class Halo:
    def __init__(self, coords, counts, rows, cols, hrow, hcol, hcor, send, recv):
        (r, c), (nr, nc) = coords, counts
        north, south = lax.rem(r + nr - 1, nr), lax.rem(r + 1, nr)
        west, east = lax.rem(c + nc - 1, nc), lax.rem(c + 1, nc)
        width = rows.shape[1]
        low, high = pl.ds(0, 16), pl.ds(width - 16, 16)
        plan = (
            (rows.at[0], hrow.at[1], (north, c)),
            (rows.at[1], hrow.at[0], (south, c)),
            (cols.at[0], hcol.at[1], (r, west)),
            (cols.at[1], hcol.at[0], (r, east)),
            (rows.at[0, low], hcor.at[3], (north, west)),
            (rows.at[0, high], hcor.at[2], (north, east)),
            (rows.at[1, low], hcor.at[1], (south, west)),
            (rows.at[1, high], hcor.at[0], (south, east)),
        )
        self.copies = [
            pltpu.make_async_remote_copy(
                src_ref=source,
                dst_ref=target,
                send_sem=send.at[k],
                recv_sem=recv.at[k],
                device_id=device,
                device_id_type=MESH,
            )
            for k, (source, target, device) in enumerate(plan)
        ]

    def start(self):
        for copy in self.copies:
            copy.start()

    def wait_recv(self):
        for copy in self.copies:
            copy.wait_recv()

    def wait_send(self):
        for copy in self.copies:
            copy.wait_send()


def put_row(field, pair, side, value, scratch):
    width = value.shape[0]
    base = side * 384
    scratch[8 : 8 + width] = value
    field[pair, :, base : base + 128] = scratch[7 : 7 + width].astype(BF)
    field[pair, :, base + 128 : base + 256] = value.astype(BF)
    field[pair, :, base + 256 : base + 384] = scratch[9 : 9 + width].astype(BF)


def set_halo(field, hrow, hcol, hcor, hcolf, masks, scratch):
    north, south, west, east = masks
    pairs, width = field.shape[0] - 1, field.shape[1]
    for pair, side, k, up in ((0, 0, 0, north), (pairs, 1, 1, south)):
        scratch[7:8] = hcor[2 * k].astype(F32)[15:16] * (up * west)
        scratch[8 + width : 9 + width] = hcor[2 * k + 1].astype(F32)[0:1] * (up * east)
        put_row(field, pair, side, hrow[k].astype(F32) * up, scratch)
    hcolf[0] = hcol[0].astype(F32) * west
    hcolf[1] = hcol[1].astype(F32) * east
    place = iota((16, 128), 0)

    def body(pair, carry):
        for half, spot, sub, lane in ((0, 0, 0, 0), (1, width - 16, 15, 256)):
            for side in (1, 0):
                at = (
                    pair + 1 - side,
                    pl.ds(spot, 16),
                    pl.ds(side * 384 + lane, 128),
                )
                cell = hcolf[half, pl.ds(2 * pair + 1 - side, 1), :]
                field[at] = jnp.where(place == sub, cell, field[at].astype(F32)).astype(BF)
        return carry

    lax.fori_loop(0, pairs, body, 0)


def take_edges(field, rows, cols, colf):
    pairs = field.shape[0] - 1
    rows[0] = field[0, :, 512:640]
    rows[1] = field[pairs, :, 128:256]
    cols[0] = colf[0].astype(BF)
    cols[1] = colf[1].astype(BF)


def windows(field, at, count):
    width = field.shape[1]
    low = field[pl.ds(at, count)].reshape(count * width, 768)
    high = field[pl.ds(at + 1, count)].reshape(count * width, 768)
    return low, high


def centres(field, at, count):
    width = field.shape[1]
    even = field[pl.ds(at, count), :, 512:640].reshape(count * width, 128)
    odd = field[pl.ds(at + 1, count), :, 128:256].reshape(count * width, 128)
    return even, odd


def pair_weights(kernel, out, flipped):
    out[...] = jnp.zeros_like(out)
    for a in range(3):
        for b in range(3):
            if flipped:
                block = kernel[(2 - a) * 3 + 2 - b].astype(F32).T.astype(BF)
            else:
                block = kernel[a * 3 + b]
            for half in range(2):
                base = (a + half) * 384 + b * 128
                out[base : base + 128, half * 128 : half * 128 + 128] = block


def tap_sums(acc, out):
    for a in range(3):
        for b in range(3):
            total = None
            for half in range(2):
                i = a + half
                lane = (i % 2) * 384 + b * 128
                part = acc[i // 2, half * 128 : half * 128 + 128, lane : lane + 128]
                total = part if total is None else total + part
            t = a * 3 + b
            out[t * 8 : t * 8 + 8] = total.T.astype(BF).reshape(8, 16, 128)


def activate(z):
    sig = 0.5 + 0.5 * jnp.tanh(0.5 * z)
    y = z * sig
    return y, sig + y * (1.0 - sig)


def kernel(counts, *refs):
    nr, nc = counts
    (ids, live, fine_h, interp_h, coarse_h, cw_h, k1_h, k2_h, c1_h, c2_h) = refs[:10]
    (skip_h, gin_h, g1_h, g2_h, gcond_h, gcoarse_h) = refs[10:16]
    (
        fine, interp, coarse, cw, k1, k2, cot1, cot2,
        skip, gin, g1, g2, gcond, gcoarse,
        field1, field2, delta1, delta2, slope, back, flip,
        w1, w2, v1, v2, cwp, cpad, table, hot, spread, perm, proj, patch,
        acc1, acc2, gpacc, shift, pool, colf, hcolf,
        ask, asked, askrow, askedrow, reply, arrived, placed, gotten, gathered,
        rows1, cols1, hrow1, hcol1, hcor1,
        rows2, cols2, hrow2, hcol2, hcor2,
        rows3, cols3, hrow3, hcol3, hcor3,
        rows4, cols4, hrow4, hcol4, hcor4,
        p1, p1in, p1mid, p1all, p1out, p2, p2in, p2mid, p2all, p2out,
        q, qin, qmid, qall, qout,
        local_sem, row_send, row_recv, col_send, col_recv, halo_send, halo_recv,
    ) = refs[16:]
    r, c = lax.axis_index("row"), lax.axis_index("col")
    here = (r, c)
    pairs1, width1 = fine.shape[0], fine.shape[2]
    pairs2, width2 = pairs1 // 2, width1 // 2
    listed = ids.shape[1]
    places = nr * SLOT
    ncoarse = coarse.shape[0]
    nblocks = ncoarse // CB

    loads = [
        pltpu.make_async_copy(source, target, local_sem.at[k])
        for k, (source, target) in enumerate(
            (
                (cw_h, cw), (coarse_h, coarse), (k1_h, k1), (interp_h, interp),
                (fine_h, fine), (k2_h, k2), (c2_h, cot2), (c1_h, cot1),
            )
        )
    ]
    for load in loads:
        load.start()

    barrier = pltpu.get_barrier_semaphore()

    def greet_row(step, carry):
        pl.semaphore_signal(barrier, inc=1, device_id=(lax.rem(r + step, nr), c), device_id_type=MESH)
        return carry

    def greet_col(step, carry):
        pl.semaphore_signal(barrier, inc=1, device_id=(r, lax.rem(c + step, nc)), device_id_type=MESH)
        return carry

    lax.fori_loop(1, nr, greet_row, 0)
    lax.fori_loop(1, nc, greet_col, 0)
    for dr in (1, nr - 1):
        for dc in (1, nc - 1):
            pl.semaphore_signal(
                barrier,
                inc=1,
                device_id=(lax.rem(r + dr, nr), lax.rem(c + dc, nc)),
                device_id_type=MESH,
            )

    live_total = live[0, 0]
    owner = [lax.shift_right_logical(ids[0, k], jnp.int32(nblocks.bit_length() - 1)) for k in range(listed)]
    local = [ids[0, k] - owner[k] * nblocks for k in range(listed)]
    place = []
    for k in range(listed):
        rank = jnp.int32(0)
        for j in range(k):
            rank = rank + jnp.where(owner[j] == owner[k], 1, 0)
        place.append(jnp.where(k < live_total, owner[k] * CAP + rank, -1))
    row_at = iota((places, 128), 0)
    row_place = lax.shift_right_logical(row_at, 3)
    row_sub = row_at - row_place * CB
    wanted = jnp.full((places, 128), -1, jnp.int32)
    for k in range(listed):
        wanted = jnp.where(row_place == place[k], local[k] * CB + row_sub, wanted)
    ask[...] = wanted.astype(F32).reshape(ask.shape)
    list_at = iota((listed * CB, 128), 0)
    list_slot = lax.shift_right_logical(list_at, 3)
    list_sub = list_at - list_slot * CB
    target = jnp.full((listed * CB, 128), -1, jnp.int32)
    for k in range(listed):
        found = jnp.where(place[k] >= 0, place[k] * CB, -CB)
        target = jnp.where(list_slot == k, found + list_sub, target)
    lanes = iota((listed * CB, 128), 1)
    for j in range(places // 128):
        perm[:, j * 128 : j * 128 + 128] = jnp.where(target == lanes + j * 128, 1.0, 0.0).astype(BF)

    pl.semaphore_wait(barrier, nr - 1 + nc - 1 + 4)

    row = lambda k, source, dest: Push(here, 0, nr, source, dest, row_send.at[k], row_recv.at[k])
    col = lambda k, source, dest: Push(here, 1, nc, source, dest, col_send.at[k], col_recv.at[k])
    halo = lambda k, *bufs: Halo(here, counts, *bufs, halo_send.at[k], halo_recv.at[k])
    masks = (
        jnp.where(r > 0, 1.0, 0.0),
        jnp.where(r < nr - 1, 1.0, 0.0),
        jnp.where(c > 0, 1.0, 0.0),
        jnp.where(c < nc - 1, 1.0, 0.0),
    )

    push_ask = row(0, lambda peer: ask.at[peer], asked)
    push_ask.start()
    asked[r] = ask[r]

    loads[0].wait()
    loads[1].wait()
    cwp[...] = jnp.zeros_like(cwp)
    cwp[0 : cw.shape[0], :] = cw[...].astype(F32)
    cpad[...] = jnp.zeros_like(cpad)
    cpad[:, 0 : coarse.shape[1]] = coarse[...]
    weight = cwp[...].astype(BF)

    def project(k, carry):
        at = pl.ds(pl.multiple_of(k * 512, 512), 512)
        part = cpad[at, :]
        table[at, 0:128] = dot(part, weight).astype(BF)
        table[at, 128:256] = part
        return carry

    lax.fori_loop(0, ncoarse // 512, project, 0)
    loads[2].wait()
    pair_weights(k1, w1, False)

    push_ask.wait_recv()
    every = asked[...].reshape(places, 128)
    lane_f = iota((places, 128), 1).astype(F32)

    def heat(k, carry):
        base = (k * 128).astype(F32)
        hot[k] = jnp.where(every == lane_f + base, 1.0, 0.0).astype(BF)
        return carry

    lax.fori_loop(0, ncoarse // 128, heat, 0)
    gathered_rows = jnp.zeros((places, 256), F32)

    def gather(k, carry):
        pieces = [hot[k * 4 + j] for j in range(4)]
        return carry + dot(
            jnp.concatenate(pieces, axis=1), table[pl.ds(pl.multiple_of(k * 512, 512), 512), :]
        )

    gathered_rows = lax.fori_loop(0, ncoarse // 512, gather, gathered_rows)
    reply[...] = gathered_rows.astype(BF).reshape(reply.shape)
    push_reply = row(1, lambda peer: reply.at[peer], arrived)
    push_reply.start()
    arrived[r] = reply[r]
    askrow[...] = every.T[0:8, :]
    push_row = col(0, lambda peer: askrow, askedrow)
    push_row.start()
    askedrow[c] = askrow[...]

    loads[5].wait()
    pair_weights(k1, v1, True)
    pair_weights(k2, w2, False)
    pair_weights(k2, v2, True)
    loads[3].wait()

    def turn(pair, carry):
        at = pl.ds(pl.multiple_of(pair * width1, width1), width1)
        for side in range(2):
            flip[side, :, at] = interp[pair, side].astype(F32).T.astype(BF)
        return carry

    lax.fori_loop(0, pairs1, turn, 0)
    shift[...] = jnp.zeros_like(shift)

    push_reply.wait_recv()
    both = dot(perm[...], arrived[...].reshape(places, 256)).astype(BF)
    proj[...] = both[:, 0:128]
    patch[...] = both[:, 128:256]
    loads[4].wait()

    def condition(k, carry):
        for j in range(4):
            pair = k * 4 + j
            value = dot(interp[pair].reshape(2 * width1, 128), proj[...])
            value = value + fine[pair].reshape(2 * width1, 128).astype(F32)
            for side in range(2):
                line = value[side * width1 : (side + 1) * width1]
                at = pl.ds(2 * pair + side, 1)
                colf[0, at, :] = line[0:1]
                colf[1, at, :] = line[width1 - 1 : width1]
                put_row(field1, pair + side, 1 - side, line, shift.at[2 * j + side])
        return carry

    lax.fori_loop(0, pairs1 // 4, condition, 0)
    take_edges(field1, rows1, cols1, colf)
    halo1 = halo(0, rows1, cols1, hrow1, hcol1, hcor1)
    halo1.start()

    push_row.wait_recv()

    def spot(k, carry):
        at = pl.ds(pl.multiple_of(k * 256, 256), 256)
        number = iota((256, places), 0).astype(F32) + (k * 256).astype(F32)
        for j in range(nc):
            match = number == askedrow[j, 0:1, :]
            spread[at, j * places : (j + 1) * places] = jnp.where(match, 1.0, 0.0).astype(BF)
        return carry

    lax.fori_loop(0, ncoarse // 256, spot, 0)

    halo1.wait_recv()
    set_halo(field1, hrow1, hcol1, hcor1, hcolf, masks, shift.at[0])

    def level_one(k, carry):
        pair = k * 4
        z = dot(jnp.concatenate(windows(field1, pair, 4), axis=1), w1[...])
        y, grade = activate(z)
        slope[pl.ds(pair, 4)] = grade.reshape(4, width1, 256)
        pool[...] = y[:, 0:128] + y[:, 128:256]
        total = pool[pl.ds(0, 4 * width2, stride=2), :] + pool[pl.ds(1, 4 * width2, stride=2), :]
        total = total * 0.25
        for j in range(4):
            line = total[j * width2 : (j + 1) * width2]
            at = pl.ds(pair + j, 1)
            colf[0, at, :] = line[0:1]
            colf[1, at, :] = line[width2 - 1 : width2]
            put_row(field2, k * 2 + (j + 1) // 2, (j + 1) % 2, line, shift.at[j])
        return carry

    lax.fori_loop(0, pairs1 // 4, level_one, 0)
    half = pl.ds(0, 2 * pairs2)
    take_edges(field2, rows2, cols2, colf.at[:, half])
    halo2 = halo(1, rows2, cols2, hrow2, hcol2, hcor2)
    halo2.start()
    loads[6].wait()
    halo2.wait_recv()
    set_halo(field2, hrow2, hcol2, hcor2, hcolf.at[:, half], masks, shift.at[0])

    def level_two(k, carry):
        pair = k * 8
        z = dot(jnp.concatenate(windows(field2, pair, 8), axis=1), w2[...])
        y, grade = activate(z)
        for side in range(2):
            lane = slice(side * 128, side * 128 + 128)
            skip[pl.ds(pair, 8), side] = y[:, lane].astype(BF).reshape(8, width2, 128)
            value = cot2[pl.ds(pair, 8), side].astype(F32) * grade[:, lane].reshape(8, width2, 128)
            for j in range(8):
                at = pl.ds(2 * (pair + j) + side, 1)
                colf[0, at, :] = value[j, 0:1]
                colf[1, at, :] = value[j, width2 - 1 : width2]
                put_row(delta2, pair + j + side, 1 - side, value[j], shift.at[j])
        return carry

    lax.fori_loop(0, pairs2 // 8, level_two, 0)
    skip_out = pltpu.make_async_copy(skip, skip_h, local_sem.at[8])
    skip_out.start()
    take_edges(delta2, rows3, cols3, colf.at[:, half])
    halo3 = halo(2, rows3, cols3, hrow3, hcol3, hcor3)
    halo3.start()

    def tap_grad(field, delta, acc, step):
        count = step // field.shape[1]

        def body(k, carry):
            outer = jnp.concatenate(centres(delta, k * count, count), axis=1)
            for i, window in enumerate(windows(field, k * count, count)):
                acc[i] += lax.dot_general(outer, window, CONTRACT0, preferred_element_type=F32)
            return carry

        acc[...] = jnp.zeros_like(acc)
        lax.fori_loop(0, (field.shape[0] - 1) // count, body, 0)

    tap_grad(field2, delta2, acc2, 1024)
    tap_sums(acc2, p2)

    class Total:
        def __init__(self, k, parts, held, middle, full):
            self.parts, self.held, self.middle, self.full = parts, held, middle, full
            self.size = parts.shape[0] // nr
            block = lambda peer: parts.at[pl.ds(peer * self.size, self.size)]
            self.first = row(k, block, held)
            self.second = col(k - 1, lambda peer: middle.at[c], middle)
            self.third = row(k + 1, lambda peer: full.at[r], full)

        def scatter(self):
            self.first.start()
            self.held[r] = self.parts[pl.ds(r * self.size, self.size)]

        def exchange(self):
            self.first.wait_recv()
            total = self.held[0].astype(F32)
            for k in range(1, nr):
                total = total + self.held[k].astype(F32)
            self.middle[c] = total.astype(self.middle.dtype)
            self.second.start()

        def gather(self):
            self.second.wait_recv()
            total = self.middle[0].astype(F32)
            for k in range(1, nc):
                total = total + self.middle[k].astype(F32)
            self.full[r] = total.astype(self.full.dtype)
            self.third.start()

        def finish(self):
            self.third.wait_recv()

        def wait_send(self):
            self.first.wait_send()
            self.second.wait_send()
            self.third.wait_send()

    sum2 = Total(2, p2, p2in, p2mid, p2all)
    sum1 = Total(4, p1, p1in, p1mid, p1all)
    sumq = Total(6, q, qin, qmid, qall)
    sum2.scatter()

    halo3.wait_recv()
    set_halo(delta2, hrow3, hcol3, hcor3, hcolf.at[:, half], masks, shift.at[0])

    def back_two(k, carry):
        z = dot(jnp.concatenate(windows(delta2, k * 8, 8), axis=1), v2[...]) * 0.25
        back[pl.ds(k * 8, 8)] = z.reshape(8, width2, 256)
        return carry

    lax.fori_loop(0, pairs2 // 8, back_two, 0)
    loads[7].wait()

    def delta_one(k, carry):
        for j in range(2):
            pair = k * 2 + j
            line = back[k, :, j * 128 : j * 128 + 128]
            base = j * width1
            pool[pl.ds(base, width2, stride=2), :] = line
            pool[pl.ds(base + 1, width2, stride=2), :] = line
            wide = pool[base : base + width1]
            for side in range(2):
                grade = slope[pair, :, side * 128 : side * 128 + 128]
                value = (cot1[pair, side].astype(F32) + wide) * grade
                at = pl.ds(2 * pair + side, 1)
                colf[0, at, :] = value[0:1]
                colf[1, at, :] = value[width1 - 1 : width1]
                put_row(delta1, pair + side, 1 - side, value, shift.at[2 * j + side])
        return carry

    lax.fori_loop(0, pairs1 // 2, delta_one, 0)
    take_edges(delta1, rows4, cols4, colf)
    halo4 = halo(3, rows4, cols4, hrow4, hcol4, hcor4)
    halo4.start()
    sum2.exchange()
    tap_grad(field1, delta1, acc1, 1024)
    tap_sums(acc1, p1)
    sum1.scatter()
    sum2.gather()
    halo4.wait_recv()
    set_halo(delta1, hrow4, hcol4, hcor4, hcolf, masks, shift.at[0])

    gpacc[...] = jnp.zeros_like(gpacc)

    def input_grad(k, carry):
        z = dot(jnp.concatenate(windows(delta1, k * 4, 4), axis=1), v1[...]).astype(BF)
        at = pl.ds(pl.multiple_of(k * 4 * width1, 4 * width1), 4 * width1)
        total = gpacc[...]
        for side in range(2):
            half_z = z[:, side * 128 : side * 128 + 128]
            gin[pl.ds(k * 4, 4), side] = half_z.reshape(4, width1, 128)
            total = total + dot(flip[side, :, at], half_z)
        gpacc[...] = total
        return carry

    lax.fori_loop(0, pairs1 // 4, input_grad, 0)
    gin_out = pltpu.make_async_copy(gin, gin_h, local_sem.at[9])
    gin_out.start()

    gproj = gpacc[...].astype(BF)
    gpatch = lax.dot_general(gproj, weight, CONTRACT1, preferred_element_type=F32).astype(BF)
    moved = lax.dot_general(perm[...], gpatch, CONTRACT0, preferred_element_type=F32)
    placed[...] = moved.astype(BF).reshape(placed.shape)
    push_back = row(8, lambda peer: placed.at[peer], gotten)
    push_back.start()
    gotten[r] = placed[r]
    q[...] = lax.dot_general(patch[...], gproj, CONTRACT0, preferred_element_type=F32).reshape(q.shape)
    sumq.scatter()
    sum1.exchange()

    push_back.wait_recv()
    gathered[c] = gotten[...]
    push_spread = col(7, lambda peer: gathered.at[c], gathered)
    push_spread.start()
    sumq.exchange()
    sum1.gather()
    sum2.finish()
    g2[...] = p2all[...].reshape(p2.shape)[0 : g2.shape[0]].astype(F32)
    g2_out = pltpu.make_async_copy(g2, g2_h, local_sem.at[10])
    g2_out.start()
    sumq.gather()
    push_spread.wait_recv()
    merged = gathered[...].reshape(nc * places, 128)

    def scatter(k, carry):
        at = pl.ds(pl.multiple_of(k * 512, 512), 512)
        gcoarse[at, :] = dot(spread[at, :], merged)[:, 0 : gcoarse.shape[1]]
        return carry

    lax.fori_loop(0, ncoarse // 512, scatter, 0)
    gcoarse_out = pltpu.make_async_copy(gcoarse, gcoarse_h, local_sem.at[11])
    gcoarse_out.start()
    sum1.finish()
    g1[...] = p1all[...].reshape(p1.shape)[0 : g1.shape[0]].astype(F32)
    g1_out = pltpu.make_async_copy(g1, g1_h, local_sem.at[12])
    g1_out.start()
    sumq.finish()
    gcond[...] = qall[...].reshape(128, 128)
    gcond_out = pltpu.make_async_copy(gcond, gcond_h, local_sem.at[13])
    gcond_out.start()

    for sent in (
        push_ask, push_reply, push_row, halo1, halo2, halo3, halo4, sum2, sum1, push_back,
        push_spread, sumq,
    ):
        sent.wait_send()
    for out in (skip_out, gin_out, g2_out, gcoarse_out, g1_out, gcond_out):
        out.wait()


def per_device(counts, fine, interp, ids, live, coarse, cw, conv_one, conv_two, cot_one, cot_two):
    nr, nc = counts
    height, width, channels = fine.shape
    pairs1, pairs2, width2 = height // 2, height // 4, width // 2
    ncoarse, cch = coarse.shape
    listed = ids.shape[-1]
    places = nr * SLOT
    blocks = -(-72 // nr) * nr
    any_space = pl.BlockSpec(memory_space=pl.ANY)
    smem = pl.BlockSpec(memory_space=pltpu.SMEM)
    vm = pltpu.VMEM
    chunk = blocks // nr

    def halo_bufs(rows, cols):
        return [
            vm((2, cols, 128), BF), vm((2, rows, 128), BF),
            vm((2, cols, 128), BF), vm((2, rows, 128), BF), vm((4, 16, 128), BF),
        ]

    def sum_bufs():
        return [
            vm((blocks, 16, 128), BF), vm((nr, chunk, 16, 128), BF), vm((nc, chunk, 16, 128), BF),
            vm((nr, chunk, 16, 128), BF),
        ]

    scratch = [
        vm((pairs1, 2, width, 128), BF), vm((pairs1, 2, width, 128), BF), vm((ncoarse, cch), BF),
        vm(cw.shape, BF), vm((9, 128, 128), BF), vm((9, 128, 128), BF),
        vm((pairs1, 2, width, 128), BF), vm((pairs2, 2, width2, 128), BF),
        vm((pairs2, 2, width2, 128), BF), vm((pairs1, 2, width, 128), BF),
        vm((72, 16, 128), F32), vm((72, 16, 128), F32), vm((128, 128), F32), vm((ncoarse, cch), F32),
        vm((pairs1 + 1, width, 768), BF), vm((pairs2 + 1, width2, 768), BF),
        vm((pairs1 + 1, width, 768), BF), vm((pairs2 + 1, width2, 768), BF),
        vm((pairs1, width, 256), F32), vm((pairs2, width2, 256), F32), vm((2, 128, pairs1 * width), BF),
        vm((1536, 256), BF), vm((1536, 256), BF), vm((1536, 256), BF), vm((1536, 256), BF),
        vm((128, 128), F32), vm((ncoarse, 128), BF), vm((ncoarse, 256), BF),
        vm((ncoarse // 128, places, 128), BF), vm((ncoarse, nc * places), BF),
        vm((listed * CB, places), BF), vm((listed * CB, 128), BF), vm((listed * CB, 128), BF),
        vm((2, 256, 768), F32), vm((2, 256, 768), F32), vm((128, 128), F32),
        vm((8, width + 16, 128), F32), vm((4 * width, 128), F32),
        vm((2, height, 128), F32), vm((2, height, 128), F32),
        vm((nr, SLOT, 128), F32), vm((nr, SLOT, 128), F32), vm((8, places), F32), vm((nc, 8, places), F32),
        vm((nr, SLOT, 256), BF), vm((nr, SLOT, 256), BF),
        vm((nr, SLOT, 128), BF), vm((nr, SLOT, 128), BF), vm((nc, nr, SLOT, 128), BF),
        *halo_bufs(height, width), *halo_bufs(height // 2, width2),
        *halo_bufs(height // 2, width2), *halo_bufs(height, width),
        *sum_bufs(), vm((8, 128), F32), *sum_bufs(), vm((8, 128), F32),
        vm((nr, 128 // nr, 128), F32), vm((nr, 1, 128 // nr, 128), F32), vm((nc, 1, 128 // nr, 128), F32),
        vm((nr, 1, 128 // nr, 128), F32), vm((8, 128), F32),
        pltpu.SemaphoreType.DMA((16,)),
        pltpu.SemaphoreType.DMA((9, nr)), pltpu.SemaphoreType.DMA((9, nr)),
        pltpu.SemaphoreType.DMA((8, nc)), pltpu.SemaphoreType.DMA((8, nc)),
        pltpu.SemaphoreType.DMA((4, 8)), pltpu.SemaphoreType.DMA((4, 8)),
    ]
    shape = jax.ShapeDtypeStruct
    skip, gin, g1, g2, gcond, gcoarse = pl.pallas_call(
        functools.partial(kernel, counts),
        out_shape=(
            shape((pairs2, 2, width2, 128), BF),
            shape((pairs1, 2, width, 128), BF),
            shape((72, 16, 128), F32),
            shape((72, 16, 128), F32),
            shape((128, 128), F32),
            shape((ncoarse, cch), F32),
        ),
        in_specs=[smem, smem] + [any_space] * 8,
        out_specs=(any_space,) * 6,
        scratch_shapes=scratch,
        compiler_params=pltpu.CompilerParams(
            collective_id=0, has_side_effects=True, vmem_limit_bytes=63 * 2**20
        ),
        cost_estimate=pl.CostEstimate(
            flops=10 * 10**9, bytes_accessed=13 * 10**6, transcendentals=2 * 10**6
        ),
    )(
        ids.reshape(1, listed),
        live.reshape(1, 1),
        fine.reshape(pairs1, 2, width, channels),
        interp.reshape(pairs1, 2, width, interp.shape[2]),
        coarse,
        cw,
        conv_one.reshape(9, 128, 128),
        conv_two.reshape(9, 128, 128),
        cot_one.reshape(pairs1, 2, width, channels),
        cot_two.reshape(pairs2, 2, width2, channels),
    )
    return (
        skip.reshape(height // 2, width2, 128),
        gin.reshape(height, width, 128),
        g1.reshape(3, 3, 128, 128),
        g2.reshape(3, 3, 128, 128),
        gcond[0:cch],
        gcoarse,
    )


def solution(mesh):
    counts = (mesh.shape["row"], mesh.shape["col"])
    tiles = P("row", "col", None)
    return jax.shard_map(
        functools.partial(per_device, counts),
        mesh=mesh,
        in_specs=(tiles, tiles, tiles, P("row", "col"), P("row", None), P(), P(), P(), tiles, tiles),
        out_specs=(tiles, tiles, P(), P(), P(), P("row", None)),
        check_vma=False,
    )
```

time: 499 us -> 99.4 us (0.20); the launches traced: 493 us -> 99.1 us
  waiting for transfers between devices: 166 us -> 0 us
  Pallas kernels: 0 us -> 86.8 us
  local copies, waits for them, and re-layouts: 96.2 us -> 11.1 us
  starting transfers between devices: 70.7 us -> 0 us
  blocking collectives: 65.6 us -> 0 us
  matrix products: 43 us -> 0 us
  other arithmetic: 34.6 us -> 0 us
  between operations: 16.2 us -> 1.3 us
    psum x2 -> x0, waiting for transfers between devices: 145 us -> none  [the longest x1 145 us: per_device(): lax.psum((grad_one, grad_two, grad_cond), ('row', 'col'))]
    pallas_call x0 -> x1, Pallas kernels: none -> 86.8 us  [per_device(): pl.pallas_call(functools.partial(kernel, counts), out_shape=(shape((pairs...]
    psum x1 -> x0, blocking collectives: 65.6 us -> none  [per_device(): lax.psum((grad_one, grad_two, grad_cond), ('row', 'col'))]
    slice x23 -> x1, local copies, waits for them, and re-layouts: 57.2 us -> 1.58 us  [per_device(): gcond[0:cch]]
    ppermute x16 -> x0, starting transfers between devices: 50.5 us -> none  [the longest x8 36.8 us: extended(): lax.ppermute(lax.slice_in_dim(block, block.shape[dim] - width, None, axis...]
    dot_general x60 -> x0, matrix products: 43 us -> none  [the longest x18 18.6 us: tap_grad(): jnp.einsum('nc,nd->cd', window, flat_delta, preferred_element_type=jnp.fl...]
    all_to_all x3 -> x0, starting transfers between devices: 20.1 us -> none  [the longest x1 8.43 us: per_device(): lax.all_to_all(request.reshape(row_count, CAP), 'row', split_axis=0, conc...]
    concatenate x7 -> x0, other arithmetic: 14.6 us -> none  [extended(): block = jnp.concatenate([low, block, high], axis=dim)]
  transfers between devices with their start and end apart: 21 -> 0, of which waited for: 9 -> 0; matrix products, arithmetic and copies ran while one was open for 8% -> 0% of each run, Pallas kernels for 0% -> 0%
where the time goes in v1:
time: 99.4 us; the launch traced here: 99.1 us
  Pallas kernels  86.8 us (87%)
  local copies, waits for them, and re-layouts  11.1 us (11%)
  between operations  1.3 us (1%)
    pallas_call x1, Pallas kernels, per_device(): pl.pallas_call(functools.partial(kernel, counts), out_shape=(shape((pairs...  86.8 us
    unnamed x12, local copies, waits for them, and re-layouts  9.47 us

profile of v1, /device:TPU:1, one launch (start us, length us, event | category | flops | bytes accessed | tf_op | source)
XLA Modules:
  0.0 99.1 jit_solution(16214850825207759982)
XLA Ops:
  1.3 2.0 %copy.16.refs_4_ = bf16[2048,100]{1,0:T(8,128)(2,1)} copy(bf16[2048,100]{0,1:T(8,128)(2,1)} %param.14) | data formatting | bytes 819200 | tf_op args[4]
  3.3 86.8 %shard_map.145 = (bf16[16,2,64,128]{3,2,1,0:T(8,128)(2,1)}, bf16[32,2,128,128]{3,2,1,0:T(8,128)(2,1)}, f32[72,16,128]{2,1,0:T(8,128)}, f32[72,16,128]{2,1,0:T(8,...) custom-call(s32[1,16]{1,0:T(1,128)} %bitcast.21, s32[1,1]{1,0:T(1,128)S(6)} %copy.22.refs_1_, ...), custom_call_target="tpu_custom_call" | custom-call | flops 10000000000 | bytes 13000000 | tf_op jit(solution)/shard_map/pallas_call | solution.py:670
  90.1 0.0 copy-start
  90.1 1.6 %slice.3 = f32[100,128]{1,0:T(8,128)} slice(f32[128,128]{1,0:T(8,128)} %get-tuple-element.16), slice={[0:100], [0:128]} | slice | bytes 102400 | tf_op jit(solution)/shard_map/slice | solution.py:706
  91.7 2.5 %copy.17 = f32[2048,100]{0,1:T(8,128)} copy(f32[2048,100]{1,0:T(8,128)} %get-tuple-element.23) | data formatting | bytes 1638400
  94.2 1.9 %copy.23 = bf16[32,64,128]{2,1,0:T(8,128)(2,1)} copy(bf16[32,64,128]{2,1,0:T(8,128)(2,1)} %bitcast.14) | data formatting | bytes 1048576
  96.0 0.0 copy-done
  96.1 0.0 copy-start.2
  96.1 0.0 copy-start.1
  96.1 1.3 %copy.24 = bf16[64,128,128]{2,1,0:T(8,128)(2,1)} copy(bf16[64,128,128]{2,1,0:T(8,128)(2,1)S(1)} %bitcast.11) | data formatting | bytes 4194304
  97.4 0.1 copy-done.2
  97.5 0.8 copy.25
  98.3 0.0 copy-done.1
  98.3 0.8 copy.26
Async XLA Ops:
  90.1 6.0 %copy-start = (bf16[32,2,128,128]{3,2,1,0:T(8,128)(2,1)S(1)}, bf16[32,2,128,128]{3,2,1,0:T(8,128)(2,1)}, u32[]{:S(2)}) copy-start(bf16[32,2,128,128]{3,2,1,0:T(8,128)(2,1)} %get-tuple-element.13) | copy-start | bytes 6291460
  96.1 1.4 %copy-start.2 = (f32[72,16,128]{2,1,0:T(8,128)S(1)}, f32[72,16,128]{2,1,0:T(8,128)}, u32[]{:S(2)}) copy-start(f32[72,16,128]{2,1,0:T(8,128)} %get-tuple-element.14) | copy-start | bytes 1769476
  96.1 2.3 %copy-start.1 = (f32[72,16,128]{2,1,0:T(8,128)S(1)}, f32[72,16,128]{2,1,0:T(8,128)}, u32[]{:S(2)}) copy-start(f32[72,16,128]{2,1,0:T(8,128)} %get-tuple-element.15) | copy-start | bytes 1769476

commit v2 on v1

--- a/solution.py
+++ b/solution.py
@@ -62,6 +62,63 @@
 
     def wait_send(self):
         self.each(lambda step: self.copy(step, self.me).wait_send())
+
+
+class Spread:
+    def __init__(self, coords, count, field, send, recv):
+        self.row, self.c = coords
+        self.field, self.send, self.recv = field, send, recv
+        self.core = lax.rem(self.c, 2)
+        self.chip = lax.div(self.c, 2)
+        self.chips = count // 2
+
+    def slot(self, step, core):
+        return lax.rem(self.chip + self.chips - step, self.chips) * 2 + core
+
+    def along(self, step):
+        peer = lax.rem(self.chip + step, self.chips) * 2 + self.core
+        return pltpu.make_async_remote_copy(
+            src_ref=self.field.at[self.c],
+            dst_ref=self.field.at[self.c],
+            send_sem=self.send.at[step],
+            recv_sem=self.recv.at[step],
+            device_id=(self.row, peer),
+            device_id_type=MESH,
+        )
+
+    def across(self, step):
+        at = self.slot(step, self.core)
+        return pltpu.make_async_remote_copy(
+            src_ref=self.field.at[at],
+            dst_ref=self.field.at[at],
+            send_sem=self.send.at[self.chips + step],
+            recv_sem=self.recv.at[self.chips + step],
+            device_id=(self.row, self.chip * 2 + 1 - self.core),
+            device_id_type=MESH,
+        )
+
+    def start(self):
+        for step in range(1, self.chips):
+            self.along(step).start()
+        self.across(0).start()
+
+    def drain(self, use):
+        steps = range(1, self.chips)
+        self.across(0).wait_recv()
+        use([self.c, self.slot(0, 1 - self.core)])
+        for step in steps:
+            self.along(step).wait_recv()
+            self.across(step).start()
+        use([self.slot(step, self.core) for step in steps])
+        for step in steps:
+            self.across(step).wait_recv()
+        use([self.slot(step, 1 - self.core) for step in steps])
+
+    def wait_send(self):
+        for step in range(1, self.chips):
+            self.along(step).wait_send()
+        for step in range(self.chips):
+            self.across(step).wait_send()
 
 
 class Halo:
@@ -198,20 +255,20 @@
 def kernel(counts, *refs):
     nr, nc = counts
     (ids, live, fine_h, interp_h, coarse_h, cw_h, k1_h, k2_h, c1_h, c2_h) = refs[:10]
-    (skip_h, gin_h, g1_h, g2_h, gcond_h, gcoarse_h) = refs[10:16]
+    (skip_h, gin_h, p1_h, p2_h, gcond_h, gcoarse_h) = refs[10:16]
     (
         fine, interp, coarse, cw, k1, k2, cot1, cot2,
-        skip, gin, g1, g2, gcond, gcoarse,
+        skip, gin, gcoarse,
         field1, field2, delta1, delta2, slope, back, flip,
-        w1, w2, v1, v2, cwp, cpad, table, hot, spread, perm, proj, patch,
-        acc1, acc2, gpacc, shift, pool, colf, hcolf,
+        w1, w2, v1, v2, cwp, coarse_t, table, hot, spread, perm, proj, patch,
+        acc1, acc2, shift, pool, colf, hcolf,
         ask, asked, askrow, askedrow, reply, arrived, placed, gotten, gathered,
         rows1, cols1, hrow1, hcol1, hcor1,
         rows2, cols2, hrow2, hcol2, hcor2,
         rows3, cols3, hrow3, hcol3, hcor3,
         rows4, cols4, hrow4, hcol4, hcor4,
-        p1, p1in, p1mid, p1all, p1out, p2, p2in, p2mid, p2all, p2out,
-        q, qin, qmid, qall, qout,
+        p1, p1in, p1mid, p1all, p2, p2in, p2mid, p2all,
+        q, qin, qmid, qall,
         local_sem, row_send, row_recv, col_send, col_recv, halo_send, halo_recv,
     ) = refs[16:]
     r, c = lax.axis_index("row"), lax.axis_index("col")
@@ -220,7 +277,7 @@
     pairs2, width2 = pairs1 // 2, width1 // 2
     listed = ids.shape[1]
     places = nr * SLOT
-    ncoarse = coarse.shape[0]
+    ncoarse = coarse.shape[1]
     nblocks = ncoarse // CB
 
     loads = [
@@ -283,6 +340,41 @@
     for j in range(places // 128):
         perm[:, j * 128 : j * 128 + 128] = jnp.where(target == lanes + j * 128, 1.0, 0.0).astype(BF)
 
+    loads[0].wait()
+    loads[1].wait()
+    cwp[...] = jnp.zeros_like(cwp)
+    cwp[0 : cw.shape[0], :] = cw[...].astype(F32)
+    coarse_t[...] = jnp.zeros_like(coarse_t)
+    weight = cwp[...].astype(BF)
+
+    def project(k, carry):
+        at = pl.ds(pl.multiple_of(k * 512, 512), 512)
+        coarse_t[0 : coarse.shape[0], :] = coarse[:, at].astype(F32)
+        part = coarse_t[...].T.astype(BF)
+        table[at, 0:128] = dot(part, weight).astype(BF)
+        table[at, 128:256] = part
+        return carry
+
+    lax.fori_loop(0, ncoarse // 512, project, 0)
+    loads[2].wait()
+    pair_weights(k1, w1, False)
+
+    loads[5].wait()
+    pair_weights(k1, v1, True)
+    pair_weights(k2, w2, False)
+    pair_weights(k2, v2, True)
+    loads[3].wait()
+
+    def turn(pair, carry):
+        at = pl.ds(pl.multiple_of(pair * width1, width1), width1)
+        for side in range(2):
+            flip[side, :, at] = interp[pair, side].astype(F32).T.astype(BF)
+        return carry
+
+    lax.fori_loop(0, pairs1, turn, 0)
+    shift[...] = jnp.zeros_like(shift)
+
+
     pl.semaphore_wait(barrier, nr - 1 + nc - 1 + 4)
 
     row = lambda k, source, dest: Push(here, 0, nr, source, dest, row_send.at[k], row_recv.at[k])
@@ -299,25 +391,6 @@
     push_ask.start()
     asked[r] = ask[r]
 
-    loads[0].wait()
-    loads[1].wait()
-    cwp[...] = jnp.zeros_like(cwp)
-    cwp[0 : cw.shape[0], :] = cw[...].astype(F32)
-    cpad[...] = jnp.zeros_like(cpad)
-    cpad[:, 0 : coarse.shape[1]] = coarse[...]
-    weight = cwp[...].astype(BF)
-
-    def project(k, carry):
-        at = pl.ds(pl.multiple_of(k * 512, 512), 512)
-        part = cpad[at, :]
-        table[at, 0:128] = dot(part, weight).astype(BF)
-        table[at, 128:256] = part
-        return carry
-
-    lax.fori_loop(0, ncoarse // 512, project, 0)
-    loads[2].wait()
-    pair_weights(k1, w1, False)
-
     push_ask.wait_recv()
     every = asked[...].reshape(places, 128)
     lane_f = iota((places, 128), 1).astype(F32)
@@ -345,21 +418,6 @@
     push_row = col(0, lambda peer: askrow, askedrow)
     push_row.start()
     askedrow[c] = askrow[...]
-
-    loads[5].wait()
-    pair_weights(k1, v1, True)
-    pair_weights(k2, w2, False)
-    pair_weights(k2, v2, True)
-    loads[3].wait()
-
-    def turn(pair, carry):
-        at = pl.ds(pl.multiple_of(pair * width1, width1), width1)
-        for side in range(2):
-            flip[side, :, at] = interp[pair, side].astype(F32).T.astype(BF)
-        return carry
-
-    lax.fori_loop(0, pairs1, turn, 0)
-    shift[...] = jnp.zeros_like(shift)
 
     push_reply.wait_recv()
     both = dot(perm[...], arrived[...].reshape(places, 256)).astype(BF)
@@ -392,7 +450,7 @@
         number = iota((256, places), 0).astype(F32) + (k * 256).astype(F32)
         for j in range(nc):
             match = number == askedrow[j, 0:1, :]
-            spread[at, j * places : (j + 1) * places] = jnp.where(match, 1.0, 0.0).astype(BF)
+            spread[j, at, :] = jnp.where(match, 1.0, 0.0).astype(BF)
         return carry
 
     lax.fori_loop(0, ncoarse // 256, spot, 0)
@@ -401,22 +459,22 @@
     set_halo(field1, hrow1, hcol1, hcor1, hcolf, masks, shift.at[0])
 
     def level_one(k, carry):
-        pair = k * 4
-        z = dot(jnp.concatenate(windows(field1, pair, 4), axis=1), w1[...])
+        pair = k * 8
+        z = dot(jnp.concatenate(windows(field1, pair, 8), axis=1), w1[...])
         y, grade = activate(z)
-        slope[pl.ds(pair, 4)] = grade.reshape(4, width1, 256)
+        slope[pl.ds(pair, 8)] = grade.reshape(8, width1, 256)
         pool[...] = y[:, 0:128] + y[:, 128:256]
-        total = pool[pl.ds(0, 4 * width2, stride=2), :] + pool[pl.ds(1, 4 * width2, stride=2), :]
+        total = pool[pl.ds(0, 8 * width2, stride=2), :] + pool[pl.ds(1, 8 * width2, stride=2), :]
         total = total * 0.25
-        for j in range(4):
+        for j in range(8):
             line = total[j * width2 : (j + 1) * width2]
             at = pl.ds(pair + j, 1)
             colf[0, at, :] = line[0:1]
             colf[1, at, :] = line[width2 - 1 : width2]
-            put_row(field2, k * 2 + (j + 1) // 2, (j + 1) % 2, line, shift.at[j])
-        return carry
-
-    lax.fori_loop(0, pairs1 // 4, level_one, 0)
+            put_row(field2, k * 4 + (j + 1) // 2, (j + 1) % 2, line, shift.at[j])
+        return carry
+
+    lax.fori_loop(0, pairs1 // 8, level_one, 0)
     half = pl.ds(0, 2 * pairs2)
     take_edges(field2, rows2, cols2, colf.at[:, half])
     halo2 = halo(1, rows2, cols2, hrow2, hcol2, hcor2)
@@ -537,31 +595,33 @@
     halo4 = halo(3, rows4, cols4, hrow4, hcol4, hcor4)
     halo4.start()
     sum2.exchange()
-    tap_grad(field1, delta1, acc1, 1024)
+    tap_grad(field1, delta1, acc1, 2048)
     tap_sums(acc1, p1)
     sum1.scatter()
     sum2.gather()
     halo4.wait_recv()
     set_halo(delta1, hrow4, hcol4, hcor4, hcolf, masks, shift.at[0])
 
-    gpacc[...] = jnp.zeros_like(gpacc)
-
     def input_grad(k, carry):
-        z = dot(jnp.concatenate(windows(delta1, k * 4, 4), axis=1), v1[...]).astype(BF)
-        at = pl.ds(pl.multiple_of(k * 4 * width1, 4 * width1), 4 * width1)
-        total = gpacc[...]
+        z = dot(jnp.concatenate(windows(delta1, k * 16, 16), axis=1), v1[...]).astype(BF)
         for side in range(2):
-            half_z = z[:, side * 128 : side * 128 + 128]
-            gin[pl.ds(k * 4, 4), side] = half_z.reshape(4, width1, 128)
-            total = total + dot(flip[side, :, at], half_z)
-        gpacc[...] = total
-        return carry
-
-    lax.fori_loop(0, pairs1 // 4, input_grad, 0)
+            gin[pl.ds(k * 16, 16), side] = z[:, side * 128 : side * 128 + 128].reshape(16, width1, 128)
+        return carry
+
+    lax.fori_loop(0, pairs1 // 16, input_grad, 0)
+
+    def list_grad(k, carry):
+        at = pl.ds(pl.multiple_of(k * 8 * width1, 8 * width1), 8 * width1)
+        for side in range(2):
+            part = gin[pl.ds(k * 8, 8), side].reshape(8 * width1, 128)
+            carry = carry + dot(flip[side, :, at], part)
+        return carry
+
+    gpacc = lax.fori_loop(0, pairs1 // 8, list_grad, jnp.zeros((128, 128), F32))
     gin_out = pltpu.make_async_copy(gin, gin_h, local_sem.at[9])
     gin_out.start()
 
-    gproj = gpacc[...].astype(BF)
+    gproj = gpacc.astype(BF)
     gpatch = lax.dot_general(gproj, weight, CONTRACT1, preferred_element_type=F32).astype(BF)
     moved = lax.dot_general(perm[...], gpatch, CONTRACT0, preferred_element_type=F32)
     placed[...] = moved.astype(BF).reshape(placed.shape)
@@ -574,33 +634,39 @@
 
     push_back.wait_recv()
     gathered[c] = gotten[...]
-    push_spread = col(7, lambda peer: gathered.at[c], gathered)
+    push_spread = Spread(here, nc, gathered, col_send.at[7], col_recv.at[7])
     push_spread.start()
     sumq.exchange()
     sum1.gather()
     sum2.finish()
-    g2[...] = p2all[...].reshape(p2.shape)[0 : g2.shape[0]].astype(F32)
-    g2_out = pltpu.make_async_copy(g2, g2_h, local_sem.at[10])
-    g2_out.start()
+    p2_out = pltpu.make_async_copy(p2all, p2_h, local_sem.at[10])
+    p2_out.start()
     sumq.gather()
-    push_spread.wait_recv()
-    merged = gathered[...].reshape(nc * places, 128)
-
-    def scatter(k, carry):
-        at = pl.ds(pl.multiple_of(k * 512, 512), 512)
-        gcoarse[at, :] = dot(spread[at, :], merged)[:, 0 : gcoarse.shape[1]]
-        return carry
-
-    lax.fori_loop(0, ncoarse // 512, scatter, 0)
+    started = []
+
+    def scatter(slots):
+        if not slots:
+            return
+        parts = jnp.concatenate([gathered[slot].reshape(places, 128) for slot in slots], axis=0)
+        first = not started
+        started.append(slots)
+
+        def body(k, carry):
+            at = pl.ds(pl.multiple_of(k * 512, 512), 512)
+            value = dot(jnp.concatenate([spread[slot, at, :] for slot in slots], axis=1), parts)
+            gcoarse[at, :] = value if first else gcoarse[at, :] + value
+            return carry
+
+        lax.fori_loop(0, ncoarse // 512, body, 0)
+
+    push_spread.drain(scatter)
     gcoarse_out = pltpu.make_async_copy(gcoarse, gcoarse_h, local_sem.at[11])
     gcoarse_out.start()
     sum1.finish()
-    g1[...] = p1all[...].reshape(p1.shape)[0 : g1.shape[0]].astype(F32)
-    g1_out = pltpu.make_async_copy(g1, g1_h, local_sem.at[12])
-    g1_out.start()
+    p1_out = pltpu.make_async_copy(p1all, p1_h, local_sem.at[12])
+    p1_out.start()
     sumq.finish()
-    gcond[...] = qall[...].reshape(128, 128)
-    gcond_out = pltpu.make_async_copy(gcond, gcond_h, local_sem.at[13])
+    gcond_out = pltpu.make_async_copy(qall, gcond_h, local_sem.at[13])
     gcond_out.start()
 
     for sent in (
@@ -608,7 +674,53 @@
         push_spread, sumq,
     ):
         sent.wait_send()
-    for out in (skip_out, gin_out, g2_out, gcoarse_out, g1_out, gcond_out):
+    for out in (skip_out, gin_out, p2_out, gcoarse_out, p1_out, gcond_out):
+        out.wait()
+
+
+def finish_kernel(skip_k, gin_k, p1_k, p2_k, gcond_k, gcoarse_k, *refs):
+    skip_h, gin_h, g1_h, g2_h, gcond_h, gcoarse_h = refs[:6]
+    skip, gin, p1, p2, qs, held, g1, g2, gcond, gcoarse, sem = refs[6:]
+    quarter = gin.shape[0] // 4
+    parts = [pl.ds(k * quarter, quarter) for k in range(4)]
+    loads = [
+        pltpu.make_async_copy(source, target, sem.at[k])
+        for k, (source, target) in enumerate(
+            (
+                (gcoarse_k, held), (skip_k, skip), (p2_k, p2), (p1_k, p1), (gcond_k, qs),
+                *((gin_k.at[part], gin.at[part]) for part in parts),
+            )
+        )
+    ]
+    for load in loads:
+        load.start()
+    outs = []
+
+    def store(source, target):
+        copy = pltpu.make_async_copy(source, target, sem.at[16 + len(outs)])
+        copy.start()
+        outs.append(copy)
+
+    loads[0].wait()
+    for k in range(held.shape[0] // 128):
+        at = slice(k * 128, k * 128 + 128)
+        gcoarse[:, at] = held[at, :].T[0 : gcoarse.shape[0], :]
+    store(gcoarse, gcoarse_h)
+    loads[1].wait()
+    store(skip, skip_h)
+    for load, part in zip(loads[5:], parts):
+        load.wait()
+        store(gin.at[part], gin_h.at[part])
+    loads[2].wait()
+    g2[...] = p2[0 : g2.shape[0]].astype(F32)
+    store(g2, g2_h)
+    loads[3].wait()
+    g1[...] = p1[0 : g1.shape[0]].astype(F32)
+    store(g1, g1_h)
+    loads[4].wait()
+    gcond[...] = qs[0 : gcond.shape[0], :]
+    store(gcond, gcond_h)
+    for out in outs:
         out.wait()
 
 
@@ -616,7 +728,7 @@
     nr, nc = counts
     height, width, channels = fine.shape
     pairs1, pairs2, width2 = height // 2, height // 4, width // 2
-    ncoarse, cch = coarse.shape
+    cch, ncoarse = coarse.shape[1], coarse.shape[0]
     listed = ids.shape[-1]
     places = nr * SLOT
     blocks = -(-72 // nr) * nr
@@ -638,44 +750,44 @@
         ]
 
     scratch = [
-        vm((pairs1, 2, width, 128), BF), vm((pairs1, 2, width, 128), BF), vm((ncoarse, cch), BF),
+        vm((pairs1, 2, width, 128), BF), vm((pairs1, 2, width, 128), BF), vm((cch, ncoarse), BF),
         vm(cw.shape, BF), vm((9, 128, 128), BF), vm((9, 128, 128), BF),
         vm((pairs1, 2, width, 128), BF), vm((pairs2, 2, width2, 128), BF),
         vm((pairs2, 2, width2, 128), BF), vm((pairs1, 2, width, 128), BF),
-        vm((72, 16, 128), F32), vm((72, 16, 128), F32), vm((128, 128), F32), vm((ncoarse, cch), F32),
+        vm((ncoarse, 128), F32),
         vm((pairs1 + 1, width, 768), BF), vm((pairs2 + 1, width2, 768), BF),
         vm((pairs1 + 1, width, 768), BF), vm((pairs2 + 1, width2, 768), BF),
         vm((pairs1, width, 256), F32), vm((pairs2, width2, 256), F32), vm((2, 128, pairs1 * width), BF),
         vm((1536, 256), BF), vm((1536, 256), BF), vm((1536, 256), BF), vm((1536, 256), BF),
-        vm((128, 128), F32), vm((ncoarse, 128), BF), vm((ncoarse, 256), BF),
-        vm((ncoarse // 128, places, 128), BF), vm((ncoarse, nc * places), BF),
+        vm((128, 128), F32), vm((128, 512), F32), vm((ncoarse, 256), BF),
+        vm((ncoarse // 128, places, 128), BF), vm((nc, ncoarse, places), BF),
         vm((listed * CB, places), BF), vm((listed * CB, 128), BF), vm((listed * CB, 128), BF),
-        vm((2, 256, 768), F32), vm((2, 256, 768), F32), vm((128, 128), F32),
-        vm((8, width + 16, 128), F32), vm((4 * width, 128), F32),
+        vm((2, 256, 768), F32), vm((2, 256, 768), F32),
+        vm((8, width + 16, 128), F32), vm((8 * width, 128), F32),
         vm((2, height, 128), F32), vm((2, height, 128), F32),
         vm((nr, SLOT, 128), F32), vm((nr, SLOT, 128), F32), vm((8, places), F32), vm((nc, 8, places), F32),
         vm((nr, SLOT, 256), BF), vm((nr, SLOT, 256), BF),
         vm((nr, SLOT, 128), BF), vm((nr, SLOT, 128), BF), vm((nc, nr, SLOT, 128), BF),
         *halo_bufs(height, width), *halo_bufs(height // 2, width2),
         *halo_bufs(height // 2, width2), *halo_bufs(height, width),
-        *sum_bufs(), vm((8, 128), F32), *sum_bufs(), vm((8, 128), F32),
+        *sum_bufs(), *sum_bufs(),
         vm((nr, 128 // nr, 128), F32), vm((nr, 1, 128 // nr, 128), F32), vm((nc, 1, 128 // nr, 128), F32),
-        vm((nr, 1, 128 // nr, 128), F32), vm((8, 128), F32),
+        vm((nr, 1, 128 // nr, 128), F32),
         pltpu.SemaphoreType.DMA((16,)),
         pltpu.SemaphoreType.DMA((9, nr)), pltpu.SemaphoreType.DMA((9, nr)),
         pltpu.SemaphoreType.DMA((8, nc)), pltpu.SemaphoreType.DMA((8, nc)),
         pltpu.SemaphoreType.DMA((4, 8)), pltpu.SemaphoreType.DMA((4, 8)),
     ]
     shape = jax.ShapeDtypeStruct
-    skip, gin, g1, g2, gcond, gcoarse = pl.pallas_call(
+    results = pl.pallas_call(
         functools.partial(kernel, counts),
         out_shape=(
             shape((pairs2, 2, width2, 128), BF),
             shape((pairs1, 2, width, 128), BF),
-            shape((72, 16, 128), F32),
-            shape((72, 16, 128), F32),
-            shape((128, 128), F32),
-            shape((ncoarse, cch), F32),
+            shape((nr, chunk, 16, 128), BF),
+            shape((nr, chunk, 16, 128), BF),
+            shape((nr, 1, 128 // nr, 128), F32),
+            shape((ncoarse, 128), F32),
         ),
         in_specs=[smem, smem] + [any_space] * 8,
         out_specs=(any_space,) * 6,
@@ -691,20 +803,48 @@
         live.reshape(1, 1),
         fine.reshape(pairs1, 2, width, channels),
         interp.reshape(pairs1, 2, width, interp.shape[2]),
-        coarse,
+        coarse.T,
         cw,
         conv_one.reshape(9, 128, 128),
         conv_two.reshape(9, 128, 128),
         cot_one.reshape(pairs1, 2, width, channels),
         cot_two.reshape(pairs2, 2, width2, channels),
     )
+    skip, gin, g1, g2, gcond, gcoarse = pl.pallas_call(
+        finish_kernel,
+        out_shape=(
+            shape((pairs2, 2, width2, 128), BF),
+            shape((pairs1, 2, width, 128), BF),
+            shape((72, 16, 128), F32),
+            shape((72, 16, 128), F32),
+            shape((cch, 128), F32),
+            shape((cch, ncoarse), F32),
+        ),
+        in_specs=[any_space] * 6,
+        out_specs=(any_space,) * 6,
+        scratch_shapes=[
+            vm((pairs2, 2, width2, 128), BF), vm((pairs1, 2, width, 128), BF),
+            vm((blocks, 16, 128), BF), vm((blocks, 16, 128), BF), vm((128, 128), F32), vm((ncoarse, 128), F32),
+            vm((72, 16, 128), F32), vm((72, 16, 128), F32), vm((cch, 128), F32), vm((cch, ncoarse), F32),
+            pltpu.SemaphoreType.DMA((32,)),
+        ],
+        compiler_params=pltpu.CompilerParams(vmem_limit_bytes=63 * 2**20),
+        cost_estimate=pl.CostEstimate(flops=0, bytes_accessed=12 * 10**6, transcendentals=0),
+    )(
+        results[0],
+        results[1],
+        results[2].reshape(blocks, 16, 128),
+        results[3].reshape(blocks, 16, 128),
+        results[4].reshape(128, 128),
+        results[5],
+    )
     return (
         skip.reshape(height // 2, width2, 128),
         gin.reshape(height, width, 128),
         g1.reshape(3, 3, 128, 128),
         g2.reshape(3, 3, 128, 128),
-        gcond[0:cch],
-        gcoarse,
+        gcond,
+        gcoarse.T,
     )
 
 

time: 99.4 us -> 88.5 us (0.89)
  local copies, waits for them, and re-layouts: 11.1 us -> 0 us
    unnamed x12 -> x0, local copies, waits for them, and re-layouts: 9.47 us -> none
    pallas_call x0 -> x1, Pallas kernels: none -> 3.99 us  [per_device(): pl.pallas_call(finish_kernel, out_shape=(shape((pairs2, 2, width2, 128),...]
    pallas_call x1, Pallas kernels: 86.8 us -> 83.1 us  [per_device(): pl.pallas_call(functools.partial(kernel, counts), out_shape=(shape((pairs...]
    slice x1 -> x0, local copies, waits for them, and re-layouts: 1.58 us -> none  [per_device(): gcond[0:cch]]
where the time goes in v2:
time: 88.5 us; the launch traced here: 88.4 us
  Pallas kernels  87.1 us (98%)
  between operations  1.29 us (1%)
    pallas_call x1, Pallas kernels, per_device(): pl.pallas_call(functools.partial(kernel, counts), out_shape=(shape((pairs...  83.1 us
    pallas_call x1, Pallas kernels, per_device(): pl.pallas_call(finish_kernel, out_shape=(shape((pairs2, 2, width2, 128),...  3.99 us

profile of v2, /device:TPU:1, one launch (start us, length us, event | category | flops | bytes accessed | tf_op | source)
XLA Modules:
  0.0 88.4 jit_solution(562489605435858273)
XLA Ops:
  1.3 83.1 %shard_map.145 = (bf16[16,2,64,128]{3,2,1,0:T(8,128)(2,1)}, bf16[32,2,128,128]{3,2,1,0:T(8,128)(2,1)}, bf16[16,5,16,128]{3,2,1,0:T(8,128)(2,1)}, bf16[16,5,16,12...) custom-call(s32[1,16]{1,0:T(1,128)} %bitcast.31, s32[1,1]{1,0:T(1,128)S(6)} %copy.16.refs_1_, ...), custom_call_target="tpu_custom_call" | custom-call | flops 10000000000 | bytes 13000000 | tf_op jit(solution)/shard_map/pallas_call | solution.py:782
  84.4 4.0 %shard_map.146 = (bf16[16,2,64,128]{3,2,1,0:T(8,128)(2,1)}, bf16[32,2,128,128]{3,2,1,0:T(8,128)(2,1)}, f32[72,16,128]{2,1,0:T(8,128)}, f32[72,16,128]{2,1,0:T(8,...) custom-call(bf16[16,2,64,128]{3,2,1,0:T(8,128)(2,1)} %get-tuple-element.18.skip_k, ...), custom_call_target="tpu_custom_call" | custom-call | bytes 12000000 | tf_op jit(solution)/shard_map/pallas_call | solution.py:813

commit v3 on v2

--- a/solution.py
+++ b/solution.py
@@ -64,60 +64,73 @@
         self.each(lambda step: self.copy(step, self.me).wait_send())
 
 
-class Spread:
-    def __init__(self, coords, count, field, send, recv):
+class Back:
+    def __init__(self, coords, counts, placed, gathered, send, recv, core_send, core_recv):
         self.row, self.c = coords
-        self.field, self.send, self.recv = field, send, recv
+        self.rows, self.chips = counts[0], counts[1] // 2
+        self.placed, self.gathered = placed, gathered
+        self.send, self.recv, self.core_send, self.core_recv = send, recv, core_send, core_recv
         self.core = lax.rem(self.c, 2)
         self.chip = lax.div(self.c, 2)
-        self.chips = count // 2
 
     def slot(self, step, core):
         return lax.rem(self.chip + self.chips - step, self.chips) * 2 + core
 
-    def along(self, step):
-        peer = lax.rem(self.chip + step, self.chips) * 2 + self.core
+    def along(self, step, place, chip_slot, row_slot):
+        row = lax.rem(self.row + place, self.rows)
+        col = lax.rem(self.chip + step, self.chips) * 2 + self.core
         return pltpu.make_async_remote_copy(
-            src_ref=self.field.at[self.c],
-            dst_ref=self.field.at[self.c],
-            send_sem=self.send.at[step],
-            recv_sem=self.recv.at[step],
-            device_id=(self.row, peer),
+            src_ref=self.placed.at[row],
+            dst_ref=self.gathered.at[chip_slot, row_slot],
+            send_sem=self.send.at[step, place],
+            recv_sem=self.recv.at[step, place],
+            device_id=(row, col),
             device_id_type=MESH,
         )
 
     def across(self, step):
         at = self.slot(step, self.core)
         return pltpu.make_async_remote_copy(
-            src_ref=self.field.at[at],
-            dst_ref=self.field.at[at],
-            send_sem=self.send.at[self.chips + step],
-            recv_sem=self.recv.at[self.chips + step],
+            src_ref=self.gathered.at[at],
+            dst_ref=self.gathered.at[at],
+            send_sem=self.core_send.at[step],
+            recv_sem=self.core_recv.at[step],
             device_id=(self.row, self.chip * 2 + 1 - self.core),
             device_id_type=MESH,
         )
 
+    def each(self, step, act):
+        def body(place, carry):
+            act(place)
+            return carry
+
+        lax.fori_loop(1 if step == 0 else 0, self.rows, body, 0)
+
     def start(self):
-        for step in range(1, self.chips):
-            self.along(step).start()
-        self.across(0).start()
-
-    def drain(self, use):
-        steps = range(1, self.chips)
-        self.across(0).wait_recv()
-        use([self.c, self.slot(0, 1 - self.core)])
-        for step in steps:
-            self.along(step).wait_recv()
+        for step in reversed(range(self.chips)):
+            self.each(step, lambda place: self.along(step, place, self.c, self.row).start())
+
+    def forward(self):
+        for step in range(self.chips):
+            at = self.slot(step, self.core)
+            self.each(
+                step,
+                lambda place: self.along(
+                    step, place, at, lax.rem(self.row + self.rows - place, self.rows)
+                ).wait_recv(),
+            )
             self.across(step).start()
-        use([self.slot(step, self.core) for step in steps])
-        for step in steps:
+
+    def slots(self, core):
+        return [self.slot(step, core) for step in range(self.chips)]
+
+    def wait_across(self):
+        for step in range(self.chips):
             self.across(step).wait_recv()
-        use([self.slot(step, 1 - self.core) for step in steps])
 
     def wait_send(self):
-        for step in range(1, self.chips):
-            self.along(step).wait_send()
         for step in range(self.chips):
+            self.each(step, lambda place: self.along(step, place, self.c, self.row).wait_send())
             self.across(step).wait_send()
 
 
@@ -261,15 +274,15 @@
         skip, gin, gcoarse,
         field1, field2, delta1, delta2, slope, back, flip,
         w1, w2, v1, v2, cwp, coarse_t, table, hot, spread, perm, proj, patch,
-        acc1, acc2, shift, pool, colf, hcolf,
-        ask, asked, askrow, askedrow, reply, arrived, placed, gotten, gathered,
+        acc1, acc2, shift, pool, stage, colf, hcolf,
+        ask, asked, askrow, askedrow, reply, arrived, placed, gathered,
         rows1, cols1, hrow1, hcol1, hcor1,
         rows2, cols2, hrow2, hcol2, hcor2,
         rows3, cols3, hrow3, hcol3, hcor3,
         rows4, cols4, hrow4, hcol4, hcor4,
         p1, p1in, p1mid, p1all, p2, p2in, p2mid, p2all,
         q, qin, qmid, qall,
-        local_sem, row_send, row_recv, col_send, col_recv, halo_send, halo_recv,
+        local_sem, row_send, row_recv, col_send, col_recv, halo_send, halo_recv, back_send, back_recv,
     ) = refs[16:]
     r, c = lax.axis_index("row"), lax.axis_index("col")
     here = (r, c)
@@ -294,24 +307,13 @@
 
     barrier = pltpu.get_barrier_semaphore()
 
-    def greet_row(step, carry):
-        pl.semaphore_signal(barrier, inc=1, device_id=(lax.rem(r + step, nr), c), device_id_type=MESH)
-        return carry
-
-    def greet_col(step, carry):
-        pl.semaphore_signal(barrier, inc=1, device_id=(r, lax.rem(c + step, nc)), device_id_type=MESH)
-        return carry
-
-    lax.fori_loop(1, nr, greet_row, 0)
-    lax.fori_loop(1, nc, greet_col, 0)
-    for dr in (1, nr - 1):
-        for dc in (1, nc - 1):
-            pl.semaphore_signal(
-                barrier,
-                inc=1,
-                device_id=(lax.rem(r + dr, nr), lax.rem(c + dc, nc)),
-                device_id_type=MESH,
-            )
+    def greet(row, col):
+        pl.semaphore_signal(barrier, inc=1, device_id=(row, col), device_id_type=MESH)
+
+    for step in range(1, nc):
+        greet(r, lax.rem(c + step, nc))
+    for step in range(1, nr):
+        greet(lax.rem(r + step, nr), c)
 
     live_total = live[0, 0]
     owner = [lax.shift_right_logical(ids[0, k], jnp.int32(nblocks.bit_length() - 1)) for k in range(listed)]
@@ -375,7 +377,7 @@
     shift[...] = jnp.zeros_like(shift)
 
 
-    pl.semaphore_wait(barrier, nr - 1 + nc - 1 + 4)
+    pl.semaphore_wait(barrier, nr - 1 + nc - 1)
 
     row = lambda k, source, dest: Push(here, 0, nr, source, dest, row_send.at[k], row_recv.at[k])
     col = lambda k, source, dest: Push(here, 1, nc, source, dest, col_send.at[k], col_recv.at[k])
@@ -425,6 +427,16 @@
     patch[...] = both[:, 128:256]
     loads[4].wait()
 
+    for half in range(2):
+        at = pl.ds(half * (width1 - 16), 16)
+        value = dot(interp[:, :, at, :].reshape(pairs1 * 32, 128), proj[...])
+        pool[...] = value + fine[:, :, at, :].reshape(pairs1 * 32, 128).astype(F32)
+        cols1[half] = pool[pl.ds(15 * half, 2 * pairs1, stride=16), :].astype(BF)
+        at = (half * (pairs1 - 1), half)
+        rows1[half] = (dot(interp[at], proj[...]) + fine[at].astype(F32)).astype(BF)
+    halo1 = halo(0, rows1, cols1, hrow1, hcol1, hcor1)
+    halo1.start()
+
     def condition(k, carry):
         for j in range(4):
             pair = k * 4 + j
@@ -432,56 +444,75 @@
             value = value + fine[pair].reshape(2 * width1, 128).astype(F32)
             for side in range(2):
                 line = value[side * width1 : (side + 1) * width1]
-                at = pl.ds(2 * pair + side, 1)
-                colf[0, at, :] = line[0:1]
-                colf[1, at, :] = line[width1 - 1 : width1]
                 put_row(field1, pair + side, 1 - side, line, shift.at[2 * j + side])
         return carry
 
     lax.fori_loop(0, pairs1 // 4, condition, 0)
-    take_edges(field1, rows1, cols1, colf)
-    halo1 = halo(0, rows1, cols1, hrow1, hcol1, hcor1)
-    halo1.start()
-
-    push_row.wait_recv()
-
-    def spot(k, carry):
-        at = pl.ds(pl.multiple_of(k * 256, 256), 256)
-        number = iota((256, places), 0).astype(F32) + (k * 256).astype(F32)
-        for j in range(nc):
-            match = number == askedrow[j, 0:1, :]
-            spread[j, at, :] = jnp.where(match, 1.0, 0.0).astype(BF)
-        return carry
-
-    lax.fori_loop(0, ncoarse // 256, spot, 0)
-
     halo1.wait_recv()
     set_halo(field1, hrow1, hcol1, hcor1, hcolf, masks, shift.at[0])
 
-    def level_one(k, carry):
-        pair = k * 8
-        z = dot(jnp.concatenate(windows(field1, pair, 8), axis=1), w1[...])
-        y, grade = activate(z)
-        slope[pl.ds(pair, 8)] = grade.reshape(8, width1, 256)
-        pool[...] = y[:, 0:128] + y[:, 128:256]
-        total = pool[pl.ds(0, 8 * width2, stride=2), :] + pool[pl.ds(1, 8 * width2, stride=2), :]
-        total = total * 0.25
-        for j in range(8):
-            line = total[j * width2 : (j + 1) * width2]
-            at = pl.ds(pair + j, 1)
-            colf[0, at, :] = line[0:1]
-            colf[1, at, :] = line[width2 - 1 : width2]
-            put_row(field2, k * 4 + (j + 1) // 2, (j + 1) % 2, line, shift.at[j])
-        return carry
-
-    lax.fori_loop(0, pairs1 // 8, level_one, 0)
-    half = pl.ds(0, 2 * pairs2)
-    take_edges(field2, rows2, cols2, colf.at[:, half])
+    middle = width1 - 32
+    inner = middle // 2
+
+    def level_one(pair, count, cols):
+        lane_rows = [field1[pl.ds(pair + j, count), cols, :].reshape(-1, 768) for j in range(2)]
+        y, grade = activate(dot(jnp.concatenate(lane_rows, axis=1), w1[...]))
+        cells = y.shape[0]
+        slope[pl.ds(pair, count), cols, :] = grade.reshape(count, cells // count, 256)
+        pool[0:cells] = y[:, 0:128] + y[:, 128:256]
+        total = pool[pl.ds(0, cells // 2, stride=2), :] + pool[pl.ds(1, cells // 2, stride=2), :]
+        return total * 0.25
+
+    for half in range(2):
+        total = level_one(0, pairs1, pl.ds(half * (width1 - 16), 16))
+        pool[0 : pairs1 * 8] = total
+        cols2[half] = pool[pl.ds(7 * half, pairs1, stride=8), :].astype(BF)
+        stage[1 : pairs1 + 1, 8 + half * (width2 - 8) : 16 + half * (width2 - 8), :] = total.reshape(
+            pairs1, 8, 128
+        )
+    for half in range(2):
+        at = half * (pairs1 - 1)
+        stage[at + 1, 16 : 16 + inner, :] = level_one(at, 1, pl.ds(16, middle))
+        rows2[half] = stage[at + 1, 8 : 8 + width2, :].astype(BF)
     halo2 = halo(1, rows2, cols2, hrow2, hcol2, hcor2)
     halo2.start()
+    step1 = (pairs1 - 2) // 3
+
+    def level_one_inner(k, carry):
+        pair = 1 + k * step1
+        total = level_one(pair, step1, pl.ds(16, middle))
+        stage[pl.ds(pair + 1, step1), 16 : 16 + inner, :] = total.reshape(step1, inner, 128)
+        return carry
+
+    lax.fori_loop(0, 3, level_one_inner, 0)
+    half = pl.ds(0, 2 * pairs2)
     loads[6].wait()
     halo2.wait_recv()
-    set_halo(field2, hrow2, hcol2, hcor2, hcolf.at[:, half], masks, shift.at[0])
+    north, south, west, east = masks
+    for k, up in ((0, north), (1, south)):
+        at = k * (pairs1 + 1)
+        stage[at, 8 : 8 + width2, :] = hrow2[k].astype(F32) * up
+        stage[at, 7:8, :] = hcor2[2 * k].astype(F32)[15:16] * (up * west)
+        stage[at, 8 + width2 : 9 + width2, :] = hcor2[2 * k + 1].astype(F32)[0:1] * (up * east)
+    hcolf[0, half] = hcol2[0].astype(F32) * west
+    hcolf[1, half] = hcol2[1].astype(F32) * east
+
+    def edge_cells(k, carry):
+        stage[k + 1, 7:8, :] = hcolf[0, pl.ds(k, 1), :]
+        stage[k + 1, 8 + width2 : 9 + width2, :] = hcolf[1, pl.ds(k, 1), :]
+        return carry
+
+    lax.fori_loop(0, pairs1, edge_cells, 0)
+
+    def lay_out(pair, carry):
+        for side in range(2):
+            for j in range(3):
+                lane = side * 384 + j * 128
+                line = stage[2 * pair + side, 7 + j : 7 + j + width2, :]
+                field2[pair, :, lane : lane + 128] = line.astype(BF)
+        return carry
+
+    lax.fori_loop(0, pairs2 + 1, lay_out, 0)
 
     def level_two(k, carry):
         pair = k * 8
@@ -516,6 +547,18 @@
 
         acc[...] = jnp.zeros_like(acc)
         lax.fori_loop(0, (field.shape[0] - 1) // count, body, 0)
+
+    push_row.wait_recv()
+
+    def spot(k, carry):
+        at = pl.ds(pl.multiple_of(k * 256, 256), 256)
+        number = iota((256, places), 0).astype(F32) + (k * 256).astype(F32)
+        for j in range(nc):
+            match = number == askedrow[j, 0:1, :]
+            spread[j, at, :] = jnp.where(match, 1.0, 0.0).astype(BF)
+        return carry
+
+    lax.fori_loop(0, ncoarse // 256, spot, 0)
 
     tap_grad(field2, delta2, acc2, 1024)
     tap_sums(acc2, p2)
@@ -622,26 +665,23 @@
     gin_out.start()
 
     gproj = gpacc.astype(BF)
+    q[...] = lax.dot_general(patch[...], gproj, CONTRACT0, preferred_element_type=F32).reshape(q.shape)
+    sumq.scatter()
     gpatch = lax.dot_general(gproj, weight, CONTRACT1, preferred_element_type=F32).astype(BF)
     moved = lax.dot_general(perm[...], gpatch, CONTRACT0, preferred_element_type=F32)
     placed[...] = moved.astype(BF).reshape(placed.shape)
-    push_back = row(8, lambda peer: placed.at[peer], gotten)
+    push_back = Back(
+        here, counts, placed, gathered, back_send, back_recv, col_send.at[7], col_recv.at[7]
+    )
     push_back.start()
-    gotten[r] = placed[r]
-    q[...] = lax.dot_general(patch[...], gproj, CONTRACT0, preferred_element_type=F32).reshape(q.shape)
-    sumq.scatter()
+    gathered[c, r] = placed[r]
     sum1.exchange()
-
-    push_back.wait_recv()
-    gathered[c] = gotten[...]
-    push_spread = Spread(here, nc, gathered, col_send.at[7], col_recv.at[7])
-    push_spread.start()
-    sumq.exchange()
-    sum1.gather()
     sum2.finish()
     p2_out = pltpu.make_async_copy(p2all, p2_h, local_sem.at[10])
     p2_out.start()
-    sumq.gather()
+    sumq.exchange()
+    push_back.forward()
+    sum1.gather()
     started = []
 
     def scatter(slots):
@@ -652,14 +692,17 @@
         started.append(slots)
 
         def body(k, carry):
-            at = pl.ds(pl.multiple_of(k * 512, 512), 512)
+            at = pl.ds(pl.multiple_of(k * 1024, 1024), 1024)
             value = dot(jnp.concatenate([spread[slot, at, :] for slot in slots], axis=1), parts)
             gcoarse[at, :] = value if first else gcoarse[at, :] + value
             return carry
 
-        lax.fori_loop(0, ncoarse // 512, body, 0)
-
-    push_spread.drain(scatter)
+        lax.fori_loop(0, ncoarse // 1024, body, 0)
+
+    scatter(push_back.slots(push_back.core))
+    sumq.gather()
+    push_back.wait_across()
+    scatter(push_back.slots(1 - push_back.core))
     gcoarse_out = pltpu.make_async_copy(gcoarse, gcoarse_h, local_sem.at[11])
     gcoarse_out.start()
     sum1.finish()
@@ -671,7 +714,7 @@
 
     for sent in (
         push_ask, push_reply, push_row, halo1, halo2, halo3, halo4, sum2, sum1, push_back,
-        push_spread, sumq,
+        sumq,
     ):
         sent.wait_send()
     for out in (skip_out, gin_out, p2_out, gcoarse_out, p1_out, gcond_out):
@@ -763,11 +806,11 @@
         vm((ncoarse // 128, places, 128), BF), vm((nc, ncoarse, places), BF),
         vm((listed * CB, places), BF), vm((listed * CB, 128), BF), vm((listed * CB, 128), BF),
         vm((2, 256, 768), F32), vm((2, 256, 768), F32),
-        vm((8, width + 16, 128), F32), vm((8 * width, 128), F32),
+        vm((8, width + 16, 128), F32), vm((8 * width, 128), F32), vm((pairs1 + 2, width2 + 16, 128), F32),
         vm((2, height, 128), F32), vm((2, height, 128), F32),
         vm((nr, SLOT, 128), F32), vm((nr, SLOT, 128), F32), vm((8, places), F32), vm((nc, 8, places), F32),
         vm((nr, SLOT, 256), BF), vm((nr, SLOT, 256), BF),
-        vm((nr, SLOT, 128), BF), vm((nr, SLOT, 128), BF), vm((nc, nr, SLOT, 128), BF),
+        vm((nr, SLOT, 128), BF), vm((nc, nr, SLOT, 128), BF),
         *halo_bufs(height, width), *halo_bufs(height // 2, width2),
         *halo_bufs(height // 2, width2), *halo_bufs(height, width),
         *sum_bufs(), *sum_bufs(),
@@ -777,6 +820,7 @@
         pltpu.SemaphoreType.DMA((9, nr)), pltpu.SemaphoreType.DMA((9, nr)),
         pltpu.SemaphoreType.DMA((8, nc)), pltpu.SemaphoreType.DMA((8, nc)),
         pltpu.SemaphoreType.DMA((4, 8)), pltpu.SemaphoreType.DMA((4, 8)),
+        pltpu.SemaphoreType.DMA((nc // 2, nr)), pltpu.SemaphoreType.DMA((nc // 2, nr)),
     ]
     shape = jax.ShapeDtypeStruct
     results = pl.pallas_call(

time: 88.5 us -> 85.2 us (0.963)
  Pallas kernels: 87.1 us -> 83.2 us
    pallas_call x1, Pallas kernels: 83.1 us -> 79.2 us  [per_device(): pl.pallas_call(functools.partial(kernel, counts), out_shape=(shape((pairs...]
where the time goes in v3:
time: 85.2 us; the launch traced here: 84.5 us
  Pallas kernels  83.2 us (98%)
  between operations  1.29 us (2%)
    pallas_call x1, Pallas kernels, per_device(): pl.pallas_call(functools.partial(kernel, counts), out_shape=(shape((pairs...  79.2 us
    pallas_call x1, Pallas kernels, per_device(): pl.pallas_call(finish_kernel, out_shape=(shape((pairs2, 2, width2, 128),...  3.99 us

profile of v3, /device:TPU:1, one launch (start us, length us, event | category | flops | bytes accessed | tf_op | source)
XLA Modules:
  0.0 84.5 jit_solution(17770982788051964607)
XLA Ops:
  1.3 79.2 %shard_map.145 = (bf16[16,2,64,128]{3,2,1,0:T(8,128)(2,1)}, bf16[32,2,128,128]{3,2,1,0:T(8,128)(2,1)}, bf16[16,5,16,128]{3,2,1,0:T(8,128)(2,1)}, bf16[16,5,16,12...) custom-call(s32[1,16]{1,0:T(1,128)} %bitcast.31, s32[1,1]{1,0:T(1,128)S(6)} %copy.16.refs_1_, ...), custom_call_target="tpu_custom_call" | custom-call | flops 10000000000 | bytes 13000000 | tf_op jit(solution)/shard_map/pallas_call | solution.py:826
  80.5 4.0 %shard_map.146 = (bf16[16,2,64,128]{3,2,1,0:T(8,128)(2,1)}, bf16[32,2,128,128]{3,2,1,0:T(8,128)(2,1)}, f32[72,16,128]{2,1,0:T(8,128)}, f32[72,16,128]{2,1,0:T(8,...) custom-call(bf16[16,2,64,128]{3,2,1,0:T(8,128)(2,1)} %get-tuple-element.18.skip_k, ...), custom_call_target="tpu_custom_call" | custom-call | bytes 12000000 | tf_op jit(solution)/shard_map/pallas_call | solution.py:857

commit v4 on v3

--- a/solution.py
+++ b/solution.py
@@ -34,14 +34,25 @@
     def device(self, index):
         return (index, self.coords[1]) if self.axis == 0 else (self.coords[0], index)
 
-    def copy(self, step, slot):
+    def copy(self, step):
         peer = lax.rem(self.me + step, self.count)
         return pltpu.make_async_remote_copy(
             src_ref=self.source(peer),
-            dst_ref=self.target.at[slot],
-            send_sem=self.send.at[step],
-            recv_sem=self.recv.at[step],
+            dst_ref=self.target.at[self.me],
+            send_sem=self.send,
+            recv_sem=self.recv,
             device_id=self.device(peer),
+            device_id_type=MESH,
+        )
+
+    def all(self):
+        blocks = self.target.at[pl.ds(0, self.count - 1)]
+        return pltpu.make_async_remote_copy(
+            src_ref=blocks,
+            dst_ref=blocks,
+            send_sem=self.send,
+            recv_sem=self.recv,
+            device_id=self.device(lax.rem(self.me + 1, self.count)),
             device_id_type=MESH,
         )
 
@@ -53,15 +64,13 @@
         lax.fori_loop(1, self.count, body, 0)
 
     def start(self):
-        self.each(lambda step: self.copy(step, self.me).start())
+        self.each(lambda step: self.copy(step).start())
 
     def wait_recv(self):
-        self.each(
-            lambda step: self.copy(step, lax.rem(self.me + self.count - step, self.count)).wait_recv()
-        )
+        self.all().wait_recv()
 
     def wait_send(self):
-        self.each(lambda step: self.copy(step, self.me).wait_send())
+        self.all().wait_send()
 
 
 class Back:
@@ -76,15 +85,26 @@
     def slot(self, step, core):
         return lax.rem(self.chip + self.chips - step, self.chips) * 2 + core
 
-    def along(self, step, place, chip_slot, row_slot):
+    def along(self, step, place):
         row = lax.rem(self.row + place, self.rows)
         col = lax.rem(self.chip + step, self.chips) * 2 + self.core
         return pltpu.make_async_remote_copy(
             src_ref=self.placed.at[row],
-            dst_ref=self.gathered.at[chip_slot, row_slot],
-            send_sem=self.send.at[step, place],
-            recv_sem=self.recv.at[step, place],
+            dst_ref=self.gathered.at[self.c, self.row],
+            send_sem=self.send.at[step],
+            recv_sem=self.recv.at[step],
             device_id=(row, col),
+            device_id_type=MESH,
+        )
+
+    def all(self, step):
+        blocks = self.placed.at[pl.ds(0, self.rows - 1 if step == 0 else self.rows)]
+        return pltpu.make_async_remote_copy(
+            src_ref=blocks,
+            dst_ref=blocks,
+            send_sem=self.send.at[step],
+            recv_sem=self.recv.at[step],
+            device_id=(lax.rem(self.row + 1, self.rows), self.c),
             device_id_type=MESH,
         )
 
@@ -108,17 +128,11 @@
 
     def start(self):
         for step in reversed(range(self.chips)):
-            self.each(step, lambda place: self.along(step, place, self.c, self.row).start())
+            self.each(step, lambda place: self.along(step, place).start())
 
     def forward(self):
         for step in range(self.chips):
-            at = self.slot(step, self.core)
-            self.each(
-                step,
-                lambda place: self.along(
-                    step, place, at, lax.rem(self.row + self.rows - place, self.rows)
-                ).wait_recv(),
-            )
+            self.all(step).wait_recv()
             self.across(step).start()
 
     def slots(self, core):
@@ -130,7 +144,7 @@
 
     def wait_send(self):
         for step in range(self.chips):
-            self.each(step, lambda place: self.along(step, place, self.c, self.row).wait_send())
+            self.all(step).wait_send()
             self.across(step).wait_send()
 
 
@@ -282,7 +296,7 @@
         rows4, cols4, hrow4, hcol4, hcor4,
         p1, p1in, p1mid, p1all, p2, p2in, p2mid, p2all,
         q, qin, qmid, qall,
-        local_sem, row_send, row_recv, col_send, col_recv, halo_send, halo_recv, back_send, back_recv,
+        local_sem, row_send, row_recv, col_send, col_recv, halo_send, halo_recv, back_send, back_recv, core_send, core_recv,
     ) = refs[16:]
     r, c = lax.axis_index("row"), lax.axis_index("col")
     here = (r, c)
@@ -671,7 +685,7 @@
     moved = lax.dot_general(perm[...], gpatch, CONTRACT0, preferred_element_type=F32)
     placed[...] = moved.astype(BF).reshape(placed.shape)
     push_back = Back(
-        here, counts, placed, gathered, back_send, back_recv, col_send.at[7], col_recv.at[7]
+        here, counts, placed, gathered, back_send, back_recv, core_send, core_recv
     )
     push_back.start()
     gathered[c, r] = placed[r]
@@ -817,10 +831,10 @@
         vm((nr, 128 // nr, 128), F32), vm((nr, 1, 128 // nr, 128), F32), vm((nc, 1, 128 // nr, 128), F32),
         vm((nr, 1, 128 // nr, 128), F32),
         pltpu.SemaphoreType.DMA((16,)),
-        pltpu.SemaphoreType.DMA((9, nr)), pltpu.SemaphoreType.DMA((9, nr)),
-        pltpu.SemaphoreType.DMA((8, nc)), pltpu.SemaphoreType.DMA((8, nc)),
+        pltpu.SemaphoreType.DMA((8,)), pltpu.SemaphoreType.DMA((8,)),
+        pltpu.SemaphoreType.DMA((7,)), pltpu.SemaphoreType.DMA((7,)),
         pltpu.SemaphoreType.DMA((4, 8)), pltpu.SemaphoreType.DMA((4, 8)),
-        pltpu.SemaphoreType.DMA((nc // 2, nr)), pltpu.SemaphoreType.DMA((nc // 2, nr)),
+        *[pltpu.SemaphoreType.DMA((nc // 2,))] * 4,
     ]
     shape = jax.ShapeDtypeStruct
     results = pl.pallas_call(

time: 85.2 us -> 79.5 us (0.933)
  Pallas kernels: 83.2 us -> 77.9 us
    pallas_call x1, Pallas kernels: 79.2 us -> 74 us  [per_device(): pl.pallas_call(functools.partial(kernel, counts), out_shape=(shape((pairs...]
where the time goes in v4:
time: 79.5 us; the launch traced here: 79.2 us
  Pallas kernels  77.9 us (98%)
  between operations  1.29 us (2%)
    pallas_call x1, Pallas kernels, per_device(): pl.pallas_call(functools.partial(kernel, counts), out_shape=(shape((pairs...  74 us
    pallas_call x1, Pallas kernels, per_device(): pl.pallas_call(finish_kernel, out_shape=(shape((pairs2, 2, width2, 128),...  3.99 us

profile of v4, /device:TPU:1, one launch (start us, length us, event | category | flops | bytes accessed | tf_op | source)
XLA Modules:
  0.0 79.2 jit_solution(13135488231541485733)
XLA Ops:
  1.3 74.0 %shard_map.145 = (bf16[16,2,64,128]{3,2,1,0:T(8,128)(2,1)}, bf16[32,2,128,128]{3,2,1,0:T(8,128)(2,1)}, bf16[16,5,16,128]{3,2,1,0:T(8,128)(2,1)}, bf16[16,5,16,12...) custom-call(s32[1,16]{1,0:T(1,128)} %bitcast.31, s32[1,1]{1,0:T(1,128)S(6)} %copy.16.refs_1_, ...), custom_call_target="tpu_custom_call" | custom-call | flops 10000000000 | bytes 13000000 | tf_op jit(solution)/shard_map/pallas_call | solution.py:840
  75.2 4.0 %shard_map.146 = (bf16[16,2,64,128]{3,2,1,0:T(8,128)(2,1)}, bf16[32,2,128,128]{3,2,1,0:T(8,128)(2,1)}, f32[72,16,128]{2,1,0:T(8,128)}, f32[72,16,128]{2,1,0:T(8,...) custom-call(bf16[16,2,64,128]{3,2,1,0:T(8,128)(2,1)} %get-tuple-element.18.skip_k, ...), custom_call_target="tpu_custom_call" | custom-call | bytes 12000000 | tf_op jit(solution)/shard_map/pallas_call | solution.py:871

commit v5 on v4

--- a/solution.py
+++ b/solution.py
@@ -165,8 +165,8 @@
             (rows.at[1, low], hcor.at[1], (south, west)),
             (rows.at[1, high], hcor.at[0], (south, east)),
         )
-        self.copies = [
-            pltpu.make_async_remote_copy(
+        def copy(source, target, k, device):
+            return pltpu.make_async_remote_copy(
                 src_ref=source,
                 dst_ref=target,
                 send_sem=send.at[k],
@@ -174,19 +174,21 @@
                 device_id=device,
                 device_id_type=MESH,
             )
-            for k, (source, target, device) in enumerate(plan)
-        ]
+
+        order = (4, 5, 6, 7, 0, 1, 2, 3)
+        self.copies = [copy(*plan[k][:2], (0, 1, 2, 2)[k // 2], plan[k][2]) for k in order]
+        self.waits = [copy(part, part, k, (north, c)) for k, part in enumerate((hrow, hcol, hcor))]
 
     def start(self):
         for copy in self.copies:
             copy.start()
 
     def wait_recv(self):
-        for copy in self.copies:
+        for copy in self.waits:
             copy.wait_recv()
 
     def wait_send(self):
-        for copy in self.copies:
+        for copy in self.waits:
             copy.wait_send()
 
 
@@ -287,7 +289,7 @@
         fine, interp, coarse, cw, k1, k2, cot1, cot2,
         skip, gin, gcoarse,
         field1, field2, delta1, delta2, slope, back, flip,
-        w1, w2, v1, v2, cwp, coarse_t, table, hot, spread, perm, proj, patch,
+        w1, w2, v1, v2, cwp, coarse_t, table, spread, perm, proj, patch,
         acc1, acc2, shift, pool, stage, colf, hcolf,
         ask, asked, askrow, askedrow, reply, arrived, placed, gathered,
         rows1, cols1, hrow1, hcol1, hcor1,
@@ -411,21 +413,14 @@
     every = asked[...].reshape(places, 128)
     lane_f = iota((places, 128), 1).astype(F32)
 
-    def heat(k, carry):
-        base = (k * 128).astype(F32)
-        hot[k] = jnp.where(every == lane_f + base, 1.0, 0.0).astype(BF)
-        return carry
-
-    lax.fori_loop(0, ncoarse // 128, heat, 0)
-    gathered_rows = jnp.zeros((places, 256), F32)
-
     def gather(k, carry):
-        pieces = [hot[k * 4 + j] for j in range(4)]
+        base = (k * 512).astype(F32)
+        pieces = [jnp.where(every == lane_f + (base + j * 128.0), 1.0, 0.0).astype(BF) for j in range(4)]
         return carry + dot(
             jnp.concatenate(pieces, axis=1), table[pl.ds(pl.multiple_of(k * 512, 512), 512), :]
         )
 
-    gathered_rows = lax.fori_loop(0, ncoarse // 512, gather, gathered_rows)
+    gathered_rows = lax.fori_loop(0, ncoarse // 512, gather, jnp.zeros((places, 256), F32))
     reply[...] = gathered_rows.astype(BF).reshape(reply.shape)
     push_reply = row(1, lambda peer: reply.at[peer], arrived)
     push_reply.start()
@@ -578,32 +573,33 @@
     tap_sums(acc2, p2)
 
     class Total:
-        def __init__(self, k, parts, held, middle, full):
+        def __init__(self, outer, inner, numbers, parts, held, middle, full):
+            (push, self.me, self.count), (cross, self.other, self.others) = outer, inner
             self.parts, self.held, self.middle, self.full = parts, held, middle, full
-            self.size = parts.shape[0] // nr
+            self.size = parts.shape[0] // self.count
             block = lambda peer: parts.at[pl.ds(peer * self.size, self.size)]
-            self.first = row(k, block, held)
-            self.second = col(k - 1, lambda peer: middle.at[c], middle)
-            self.third = row(k + 1, lambda peer: full.at[r], full)
+            self.first = push(numbers[0], block, held)
+            self.second = cross(numbers[1], lambda peer: middle.at[self.other], middle)
+            self.third = push(numbers[2], lambda peer: full.at[self.me], full)
 
         def scatter(self):
             self.first.start()
-            self.held[r] = self.parts[pl.ds(r * self.size, self.size)]
+            self.held[self.me] = self.parts[pl.ds(self.me * self.size, self.size)]
 
         def exchange(self):
             self.first.wait_recv()
             total = self.held[0].astype(F32)
-            for k in range(1, nr):
+            for k in range(1, self.count):
                 total = total + self.held[k].astype(F32)
-            self.middle[c] = total.astype(self.middle.dtype)
+            self.middle[self.other] = total.astype(self.middle.dtype)
             self.second.start()
 
         def gather(self):
             self.second.wait_recv()
             total = self.middle[0].astype(F32)
-            for k in range(1, nc):
+            for k in range(1, self.others):
                 total = total + self.middle[k].astype(F32)
-            self.full[r] = total.astype(self.full.dtype)
+            self.full[self.me] = total.astype(self.full.dtype)
             self.third.start()
 
         def finish(self):
@@ -614,9 +610,10 @@
             self.second.wait_send()
             self.third.wait_send()
 
-    sum2 = Total(2, p2, p2in, p2mid, p2all)
-    sum1 = Total(4, p1, p1in, p1mid, p1all)
-    sumq = Total(6, q, qin, qmid, qall)
+    over_row, over_col = (row, r, nr), (col, c, nc)
+    sum2 = Total(over_row, over_col, (2, 1, 3), p2, p2in, p2mid, p2all)
+    sum1 = Total(over_row, over_col, (4, 3, 5), p1, p1in, p1mid, p1all)
+    sumq = Total(over_col, over_row, (5, 6, 6), q, qin, qmid, qall)
     sum2.scatter()
 
     halo3.wait_recv()
@@ -744,8 +741,8 @@
         pltpu.make_async_copy(source, target, sem.at[k])
         for k, (source, target) in enumerate(
             (
-                (gcoarse_k, held), (skip_k, skip), (p2_k, p2), (p1_k, p1), (gcond_k, qs),
-                *((gin_k.at[part], gin.at[part]) for part in parts),
+                (gcoarse_k, held), *((gin_k.at[part], gin.at[part]) for part in parts),
+                (skip_k, skip), (p2_k, p2), (p1_k, p1), (gcond_k, qs),
             )
         )
     ]
@@ -759,22 +756,23 @@
         outs.append(copy)
 
     loads[0].wait()
-    for k in range(held.shape[0] // 128):
-        at = slice(k * 128, k * 128 + 128)
-        gcoarse[:, at] = held[at, :].T[0 : gcoarse.shape[0], :]
+    pieces = held.shape[0] // 4
+    for j, part in enumerate(parts):
+        loads[1 + j].wait()
+        store(gin.at[part], gin_h.at[part])
+        for k in range(pieces // 128):
+            at = slice(j * pieces + k * 128, j * pieces + k * 128 + 128)
+            gcoarse[:, at] = held[at, :].T[0 : gcoarse.shape[0], :]
     store(gcoarse, gcoarse_h)
-    loads[1].wait()
+    loads[5].wait()
     store(skip, skip_h)
-    for load, part in zip(loads[5:], parts):
-        load.wait()
-        store(gin.at[part], gin_h.at[part])
-    loads[2].wait()
+    loads[6].wait()
     g2[...] = p2[0 : g2.shape[0]].astype(F32)
     store(g2, g2_h)
-    loads[3].wait()
+    loads[7].wait()
     g1[...] = p1[0 : g1.shape[0]].astype(F32)
     store(g1, g1_h)
-    loads[4].wait()
+    loads[8].wait()
     gcond[...] = qs[0 : gcond.shape[0], :]
     store(gcond, gcond_h)
     for out in outs:
@@ -817,7 +815,7 @@
         vm((pairs1, width, 256), F32), vm((pairs2, width2, 256), F32), vm((2, 128, pairs1 * width), BF),
         vm((1536, 256), BF), vm((1536, 256), BF), vm((1536, 256), BF), vm((1536, 256), BF),
         vm((128, 128), F32), vm((128, 512), F32), vm((ncoarse, 256), BF),
-        vm((ncoarse // 128, places, 128), BF), vm((nc, ncoarse, places), BF),
+        vm((nc, ncoarse, places), BF),
         vm((listed * CB, places), BF), vm((listed * CB, 128), BF), vm((listed * CB, 128), BF),
         vm((2, 256, 768), F32), vm((2, 256, 768), F32),
         vm((8, width + 16, 128), F32), vm((8 * width, 128), F32), vm((pairs1 + 2, width2 + 16, 128), F32),
@@ -828,12 +826,12 @@
         *halo_bufs(height, width), *halo_bufs(height // 2, width2),
         *halo_bufs(height // 2, width2), *halo_bufs(height, width),
         *sum_bufs(), *sum_bufs(),
-        vm((nr, 128 // nr, 128), F32), vm((nr, 1, 128 // nr, 128), F32), vm((nc, 1, 128 // nr, 128), F32),
-        vm((nr, 1, 128 // nr, 128), F32),
+        vm((nc, 128 // nc, 128), F32), vm((nc, 1, 128 // nc, 128), F32), vm((nr, 1, 128 // nc, 128), F32),
+        vm((nc, 1, 128 // nc, 128), F32),
         pltpu.SemaphoreType.DMA((16,)),
         pltpu.SemaphoreType.DMA((8,)), pltpu.SemaphoreType.DMA((8,)),
         pltpu.SemaphoreType.DMA((7,)), pltpu.SemaphoreType.DMA((7,)),
-        pltpu.SemaphoreType.DMA((4, 8)), pltpu.SemaphoreType.DMA((4, 8)),
+        pltpu.SemaphoreType.DMA((4, 3)), pltpu.SemaphoreType.DMA((4, 3)),
         *[pltpu.SemaphoreType.DMA((nc // 2,))] * 4,
     ]
     shape = jax.ShapeDtypeStruct
@@ -844,7 +842,7 @@
             shape((pairs1, 2, width, 128), BF),
             shape((nr, chunk, 16, 128), BF),
             shape((nr, chunk, 16, 128), BF),
-            shape((nr, 1, 128 // nr, 128), F32),
+            shape((nc, 1, 128 // nc, 128), F32),
             shape((ncoarse, 128), F32),
         ),
         in_specs=[smem, smem] + [any_space] * 8,

time: 79.5 us -> 77.3 us (0.972)
  Pallas kernels: 77.9 us -> 75.9 us
    pallas_call x1, Pallas kernels: 74 us -> 72.1 us  [per_device(): pl.pallas_call(functools.partial(kernel, counts), out_shape=(shape((pairs...]
where the time goes in v5:
time: 77.3 us; the launch traced here: 77.2 us
  Pallas kernels  75.9 us (98%)
  between operations  1.29 us (2%)
    pallas_call x1, Pallas kernels, per_device(): pl.pallas_call(functools.partial(kernel, counts), out_shape=(shape((pairs...  72.1 us
    pallas_call x1, Pallas kernels, per_device(): pl.pallas_call(finish_kernel, out_shape=(shape((pairs2, 2, width2, 128),...  3.79 us

profile of v5, /device:TPU:1, one launch (start us, length us, event | category | flops | bytes accessed | tf_op | source)
XLA Modules:
  0.0 77.2 jit_solution(480988893605859208)
XLA Ops:
  1.3 72.1 %shard_map.145 = (bf16[16,2,64,128]{3,2,1,0:T(8,128)(2,1)}, bf16[32,2,128,128]{3,2,1,0:T(8,128)(2,1)}, bf16[16,5,16,128]{3,2,1,0:T(8,128)(2,1)}, bf16[16,5,16,12...) custom-call(s32[1,16]{1,0:T(1,128)} %bitcast.31, s32[1,1]{1,0:T(1,128)S(6)} %copy.16.refs_1_, ...), custom_call_target="tpu_custom_call" | custom-call | flops 10000000000 | bytes 13000000 | tf_op jit(solution)/shard_map/pallas_call | solution.py:838
  73.4 3.8 %shard_map.146 = (bf16[16,2,64,128]{3,2,1,0:T(8,128)(2,1)}, bf16[32,2,128,128]{3,2,1,0:T(8,128)(2,1)}, f32[72,16,128]{2,1,0:T(8,128)}, f32[72,16,128]{2,1,0:T(8,...) custom-call(bf16[16,2,64,128]{3,2,1,0:T(8,128)(2,1)} %get-tuple-element.18.skip_k, ...), custom_call_target="tpu_custom_call" | custom-call | bytes 12000000 | tf_op jit(solution)/shard_map/pallas_call | solution.py:869

commit v6 on v5

--- a/solution.py
+++ b/solution.py
@@ -358,41 +358,6 @@
     for j in range(places // 128):
         perm[:, j * 128 : j * 128 + 128] = jnp.where(target == lanes + j * 128, 1.0, 0.0).astype(BF)
 
-    loads[0].wait()
-    loads[1].wait()
-    cwp[...] = jnp.zeros_like(cwp)
-    cwp[0 : cw.shape[0], :] = cw[...].astype(F32)
-    coarse_t[...] = jnp.zeros_like(coarse_t)
-    weight = cwp[...].astype(BF)
-
-    def project(k, carry):
-        at = pl.ds(pl.multiple_of(k * 512, 512), 512)
-        coarse_t[0 : coarse.shape[0], :] = coarse[:, at].astype(F32)
-        part = coarse_t[...].T.astype(BF)
-        table[at, 0:128] = dot(part, weight).astype(BF)
-        table[at, 128:256] = part
-        return carry
-
-    lax.fori_loop(0, ncoarse // 512, project, 0)
-    loads[2].wait()
-    pair_weights(k1, w1, False)
-
-    loads[5].wait()
-    pair_weights(k1, v1, True)
-    pair_weights(k2, w2, False)
-    pair_weights(k2, v2, True)
-    loads[3].wait()
-
-    def turn(pair, carry):
-        at = pl.ds(pl.multiple_of(pair * width1, width1), width1)
-        for side in range(2):
-            flip[side, :, at] = interp[pair, side].astype(F32).T.astype(BF)
-        return carry
-
-    lax.fori_loop(0, pairs1, turn, 0)
-    shift[...] = jnp.zeros_like(shift)
-
-
     pl.semaphore_wait(barrier, nr - 1 + nc - 1)
 
     row = lambda k, source, dest: Push(here, 0, nr, source, dest, row_send.at[k], row_recv.at[k])
@@ -409,6 +374,31 @@
     push_ask.start()
     asked[r] = ask[r]
 
+    loads[0].wait()
+    loads[1].wait()
+    cwp[...] = jnp.zeros_like(cwp)
+    cwp[0 : cw.shape[0], :] = cw[...].astype(F32)
+    coarse_t[...] = jnp.zeros_like(coarse_t)
+    weight = cwp[...].astype(BF)
+
+    def project(k, carry):
+        at = pl.ds(pl.multiple_of(k * 512, 512), 512)
+        coarse_t[0 : coarse.shape[0], :] = coarse[:, at].astype(F32)
+        part = coarse_t[...].T.astype(BF)
+        table[at, 0:128] = dot(part, weight).astype(BF)
+        table[at, 128:256] = part
+        return carry
+
+    lax.fori_loop(0, ncoarse // 512, project, 0)
+    loads[2].wait()
+    pair_weights(k1, w1, False)
+
+    loads[5].wait()
+    pair_weights(k1, v1, True)
+    pair_weights(k2, w2, False)
+    pair_weights(k2, v2, True)
+    shift[...] = jnp.zeros_like(shift)
+
     push_ask.wait_recv()
     every = asked[...].reshape(places, 128)
     lane_f = iota((places, 128), 1).astype(F32)
@@ -429,6 +419,16 @@
     push_row = col(0, lambda peer: askrow, askedrow)
     push_row.start()
     askedrow[c] = askrow[...]
+
+    loads[3].wait()
+
+    def turn(pair, carry):
+        at = pl.ds(pl.multiple_of(pair * width1, width1), width1)
+        for side in range(2):
+            flip[side, :, at] = interp[pair, side].astype(F32).T.astype(BF)
+        return carry
+
+    lax.fori_loop(0, pairs1, turn, 0)
 
     push_reply.wait_recv()
     both = dot(perm[...], arrived[...].reshape(places, 256)).astype(BF)

time: 77.3 us -> 75.4 us (0.975)
  Pallas kernels: 75.9 us -> 74 us
    pallas_call x1, Pallas kernels: 72.1 us -> 70.2 us  [per_device(): pl.pallas_call(functools.partial(kernel, counts), out_shape=(shape((pairs...]
where the time goes in v6:
time: 75.4 us; the launch traced here: 75.3 us
  Pallas kernels  74 us (98%)
  between operations  1.29 us (2%)
    pallas_call x1, Pallas kernels, per_device(): pl.pallas_call(functools.partial(kernel, counts), out_shape=(shape((pairs...  70.2 us
    pallas_call x1, Pallas kernels, per_device(): pl.pallas_call(finish_kernel, out_shape=(shape((pairs2, 2, width2, 128),...  3.79 us

profile of v6, /device:TPU:1, one launch (start us, length us, event | category | flops | bytes accessed | tf_op | source)
XLA Modules:
  0.0 75.3 jit_solution(10345073814757169722)
XLA Ops:
  1.3 70.2 %shard_map.145 = (bf16[16,2,64,128]{3,2,1,0:T(8,128)(2,1)}, bf16[32,2,128,128]{3,2,1,0:T(8,128)(2,1)}, bf16[16,5,16,128]{3,2,1,0:T(8,128)(2,1)}, bf16[16,5,16,12...) custom-call(s32[1,16]{1,0:T(1,128)} %bitcast.31, s32[1,1]{1,0:T(1,128)S(6)} %copy.16.refs_1_, ...), custom_call_target="tpu_custom_call" | custom-call | flops 10000000000 | bytes 13000000 | tf_op jit(solution)/shard_map/pallas_call | solution.py:838
  71.5 3.8 %shard_map.146 = (bf16[16,2,64,128]{3,2,1,0:T(8,128)(2,1)}, bf16[32,2,128,128]{3,2,1,0:T(8,128)(2,1)}, f32[72,16,128]{2,1,0:T(8,128)}, f32[72,16,128]{2,1,0:T(8,...) custom-call(bf16[16,2,64,128]{3,2,1,0:T(8,128)(2,1)} %get-tuple-element.18.skip_k, ...), custom_call_target="tpu_custom_call" | custom-call | bytes 12000000 | tf_op jit(solution)/shard_map/pallas_call | solution.py:869

commit v7 on v6

--- a/solution.py
+++ b/solution.py
@@ -309,6 +309,16 @@
     ncoarse = coarse.shape[1]
     nblocks = ncoarse // CB
 
+    barrier = pltpu.get_barrier_semaphore()
+
+    def greet(row, col):
+        pl.semaphore_signal(barrier, inc=1, device_id=(row, col), device_id_type=MESH)
+
+    for step in range(1, nc):
+        greet(r, lax.rem(c + step, nc))
+    for step in range(1, nr):
+        greet(lax.rem(r + step, nr), c)
+
     loads = [
         pltpu.make_async_copy(source, target, local_sem.at[k])
         for k, (source, target) in enumerate(
@@ -320,16 +330,6 @@
     ]
     for load in loads:
         load.start()
-
-    barrier = pltpu.get_barrier_semaphore()
-
-    def greet(row, col):
-        pl.semaphore_signal(barrier, inc=1, device_id=(row, col), device_id_type=MESH)
-
-    for step in range(1, nc):
-        greet(r, lax.rem(c + step, nc))
-    for step in range(1, nr):
-        greet(lax.rem(r + step, nr), c)
 
     live_total = live[0, 0]
     owner = [lax.shift_right_logical(ids[0, k], jnp.int32(nblocks.bit_length() - 1)) for k in range(listed)]
@@ -347,6 +347,22 @@
     for k in range(listed):
         wanted = jnp.where(row_place == place[k], local[k] * CB + row_sub, wanted)
     ask[...] = wanted.astype(F32).reshape(ask.shape)
+    pl.semaphore_wait(barrier, nr - 1 + nc - 1)
+
+    row = lambda k, source, dest: Push(here, 0, nr, source, dest, row_send.at[k], row_recv.at[k])
+    col = lambda k, source, dest: Push(here, 1, nc, source, dest, col_send.at[k], col_recv.at[k])
+    halo = lambda k, *bufs: Halo(here, counts, *bufs, halo_send.at[k], halo_recv.at[k])
+    masks = (
+        jnp.where(r > 0, 1.0, 0.0),
+        jnp.where(r < nr - 1, 1.0, 0.0),
+        jnp.where(c > 0, 1.0, 0.0),
+        jnp.where(c < nc - 1, 1.0, 0.0),
+    )
+
+    push_ask = row(0, lambda peer: ask.at[peer], asked)
+    push_ask.start()
+    asked[r] = ask[r]
+
     list_at = iota((listed * CB, 128), 0)
     list_slot = lax.shift_right_logical(list_at, 3)
     list_sub = list_at - list_slot * CB
@@ -357,22 +373,6 @@
     lanes = iota((listed * CB, 128), 1)
     for j in range(places // 128):
         perm[:, j * 128 : j * 128 + 128] = jnp.where(target == lanes + j * 128, 1.0, 0.0).astype(BF)
-
-    pl.semaphore_wait(barrier, nr - 1 + nc - 1)
-
-    row = lambda k, source, dest: Push(here, 0, nr, source, dest, row_send.at[k], row_recv.at[k])
-    col = lambda k, source, dest: Push(here, 1, nc, source, dest, col_send.at[k], col_recv.at[k])
-    halo = lambda k, *bufs: Halo(here, counts, *bufs, halo_send.at[k], halo_recv.at[k])
-    masks = (
-        jnp.where(r > 0, 1.0, 0.0),
-        jnp.where(r < nr - 1, 1.0, 0.0),
-        jnp.where(c > 0, 1.0, 0.0),
-        jnp.where(c < nc - 1, 1.0, 0.0),
-    )
-
-    push_ask = row(0, lambda peer: ask.at[peer], asked)
-    push_ask.start()
-    asked[r] = ask[r]
 
     loads[0].wait()
     loads[1].wait()

time: 75.4 us -> 75.6 us (level)
  no operation moved by 1% of the time
where the time goes in v7:
time: 75.6 us; the launch traced here: 75.4 us
  Pallas kernels  74.2 us (98%)
  between operations  1.29 us (2%)
    pallas_call x1, Pallas kernels, per_device(): pl.pallas_call(functools.partial(kernel, counts), out_shape=(shape((pairs...  70.4 us
    pallas_call x1, Pallas kernels, per_device(): pl.pallas_call(finish_kernel, out_shape=(shape((pairs2, 2, width2, 128),...  3.79 us

profile of v7, /device:TPU:1, one launch (start us, length us, event | category | flops | bytes accessed | tf_op | source)
XLA Modules:
  0.0 75.4 jit_solution(6564276650395092416)
XLA Ops:
  1.3 70.4 %shard_map.145 = (bf16[16,2,64,128]{3,2,1,0:T(8,128)(2,1)}, bf16[32,2,128,128]{3,2,1,0:T(8,128)(2,1)}, bf16[16,5,16,128]{3,2,1,0:T(8,128)(2,1)}, bf16[16,5,16,12...) custom-call(s32[1,16]{1,0:T(1,128)} %bitcast.31, s32[1,1]{1,0:T(1,128)S(6)} %copy.16.refs_1_, ...), custom_call_target="tpu_custom_call" | custom-call | flops 10000000000 | bytes 13000000 | tf_op jit(solution)/shard_map/pallas_call | solution.py:838
  71.6 3.8 %shard_map.146 = (bf16[16,2,64,128]{3,2,1,0:T(8,128)(2,1)}, bf16[32,2,128,128]{3,2,1,0:T(8,128)(2,1)}, f32[72,16,128]{2,1,0:T(8,128)}, f32[72,16,128]{2,1,0:T(8,...) custom-call(bf16[16,2,64,128]{3,2,1,0:T(8,128)(2,1)} %get-tuple-element.18.skip_k, ...), custom_call_target="tpu_custom_call" | custom-call | bytes 12000000 | tf_op jit(solution)/shard_map/pallas_call | solution.py:869
